TPU v7x, 32 devices: a whole 2x2x4 slice. The times are simulated.
32 devices in a mesh: dp: 16 (over z, x, core), tensor: 2 (over y).
Axes of the slice: x: 2, y: 2, z: 4, core: 2. Of those that a mesh axis runs over, the one named last changes fastest.
Arguments:
- frames: bfloat16 [16, 1500, 1280], P('dp', 'tensor'), may hold values from -6 to 6
- frame_counts: int32 [16], P('dp'), may hold values from 2 to 1500
- encoder_gain: float32 [1280], replicated, may hold values from 0.25 to 1.75
- encoder_shift: float32 [1280], replicated, may hold values from -3 to 3
- encoder_qkv: bfloat16 [3, 1280, 640], P(None, 'dp', 'tensor'), may hold values from -0.25 to 0.25
- encoder_out: bfloat16 [640, 1280], P('tensor', 'dp'), may hold values from -0.25 to 0.25
- post_gain: float32 [1280], replicated, may hold values from 0.25 to 1.75
- post_shift: float32 [1280], replicated, may hold values from -3 to 3
- projector: bfloat16 [1280, 2048], P('dp', 'tensor'), may hold values from -0.15625 to 0.15625
- projector_shift: float32 [2048], replicated, may hold values from -3 to 3
- text_embed: bfloat16 [16, 42, 2048], P('dp', 'tensor'), may hold values from -6 to 6
- decoder_gain: float32 [2048], replicated, may hold values from 0.25 to 1.75
- decoder_qkv: bfloat16 [3, 2048, 2048], P(None, 'dp', 'tensor'), may hold values from -0.25 to 0.25
- adapter_in: float32 [2, 2048, 64], replicated, may hold values from -0.125 to 0.125
- adapter_out: float32 [2, 64, 2048], P(None, None, 'tensor'), may hold values from -0.75 to 0.75
- audio_upstream: bfloat16 [16, 750, 2048], P('dp', None, 'tensor'), may hold values from -0.29882812 to 0.29882812
- text_upstream: bfloat16 [16, 42, 2048], P('dp', None, 'tensor'), may hold values from -0.29882812 to 0.29882812
Outputs:
- adapter_in_grad: float32 [2, 2048, 64], P(None, ('dp', 'tensor'))
- adapter_out_grad: float32 [2, 64, 2048], P(None, 'dp', 'tensor')
All inputs are finite; a program needn't handle non-finite values.
Results may differ from a plain program's by a relative error of at most 0.034.
Values may be sent and summed in bfloat16 or wider, within the bound.
A program may use at most 128 MiB of HBM per device.

v0:
```python
import jax
import jax.numpy as jnp
from jax import lax
from jax.sharding import PartitionSpec as P

EHD = 64
HD = 128


EPS_LAYER = 1e-05
EPS_ROOT = 1e-06
ADAPTER_SCALE = 2.0
ROPE_BASE = 10000.0
HIGHEST = lax.Precision.HIGHEST


def layer_norm(values, gain, shift):
    values = values.astype(jnp.float32)
    center = values - jnp.mean(values, -1, keepdims=True)
    spread = jnp.mean(center * center, -1, keepdims=True)
    return center * lax.rsqrt(spread + EPS_LAYER) * gain + shift


def root_norm(values, gain):
    values = values.astype(jnp.float32)
    return (
        values * lax.rsqrt(jnp.mean(values * values, -1, keepdims=True) + EPS_ROOT) * gain
    ).astype(jnp.bfloat16)


def encoder_head(queries, keys_in, values_in, usable):
    scores = jnp.dot(queries, keys_in.T, preferred_element_type=jnp.float32) * queries.shape[
        -1
    ] ** (-0.5)
    scores = jnp.where(usable[None, :], scores, -jnp.inf)
    row_top = jnp.max(scores, -1, keepdims=True)
    weights = jnp.exp(scores - row_top)
    probabilities = (weights / jnp.sum(weights, -1, keepdims=True)).astype(jnp.bfloat16)
    return jnp.dot(probabilities, values_in, preferred_element_type=jnp.float32).astype(
        jnp.bfloat16
    )


def encoder_attention(queries, keys_in, values_in, usable, head_width):
    length = queries.shape[0]

    def heads_first(array_in):
        return array_in.reshape(array_in.shape[0], -1, head_width).transpose(1, 0, 2)

    context = lax.map(
        lambda members: encoder_head(members[0], members[1], members[2], usable),
        (heads_first(queries), heads_first(keys_in), heads_first(values_in)),
    )
    return context.transpose(1, 0, 2).reshape(length, -1)


def rope_tables(length, head_width):
    position = jnp.arange(length).astype(jnp.float32)
    frequency = ROPE_BASE ** (-jnp.arange(0, head_width, 2).astype(jnp.float32) / head_width)
    angles = position[:, None] * frequency[None, :]
    angles = jnp.concatenate([angles, angles], -1)
    return (jnp.cos(angles)[:, None, :], jnp.sin(angles)[:, None, :])


def rotate(values, cosine, sine_table):
    half_width = values.shape[-1] // 2
    turned = jnp.concatenate([-values[..., half_width:], values[..., :half_width]], -1)
    return values * cosine + turned * sine_table


def unrotate(grad_rows, cosine, sine_table):
    half_width = grad_rows.shape[-1] // 2
    scaled = grad_rows * sine_table
    back_part = jnp.concatenate([scaled[..., half_width:], -scaled[..., :half_width]], -1)
    return grad_rows * cosine + back_part


def decoder_head(queries, keys_in, values_in, upstream, allowed):
    score_scale = queries.shape[-1] ** (-0.5)
    scores = jnp.dot(queries, keys_in.T, preferred_element_type=jnp.float32) * score_scale
    scores = jnp.where(allowed, scores, -jnp.inf)
    row_top = jnp.max(scores, -1, keepdims=True)
    weights = jnp.exp(scores - row_top)
    probabilities = weights / jnp.sum(weights, -1, keepdims=True)
    rounded = probabilities.astype(jnp.bfloat16)
    context = jnp.dot(rounded, values_in, preferred_element_type=jnp.float32).astype(jnp.bfloat16)
    row_delta = jnp.sum(
        upstream.astype(jnp.float32) * context.astype(jnp.float32), -1, keepdims=True
    )
    grad_probs = jnp.dot(upstream, values_in.T, preferred_element_type=jnp.float32)
    grad_scores = (probabilities * (grad_probs - row_delta) * score_scale).astype(jnp.bfloat16)
    grad_query = jnp.dot(grad_scores, keys_in, preferred_element_type=jnp.float32)
    grad_value = jnp.dot(rounded.T, upstream, preferred_element_type=jnp.float32)
    return (grad_query, grad_value)


def adapter_grads(
    normed,
    query_base,
    key_base,
    value_base,
    upstream,
    frame_count,
    audio_total,
    adapter_in,
    adapter_out,
    head_width,
):
    length = normed.shape[0]
    full_rows = normed.astype(jnp.float32)
    low_query = jnp.dot(full_rows, adapter_in[0], precision=HIGHEST)
    low_value = jnp.dot(full_rows, adapter_in[1], precision=HIGHEST)
    queries = query_base + ADAPTER_SCALE * jnp.dot(low_query, adapter_out[0], precision=HIGHEST)
    values_in = value_base + ADAPTER_SCALE * jnp.dot(low_value, adapter_out[1], precision=HIGHEST)
    cosine, sine_table = rope_tables(length, head_width)
    queries = rotate(queries.reshape(length, -1, head_width), cosine, sine_table).astype(
        jnp.bfloat16
    )
    keys_in = rotate(key_base.reshape(length, -1, head_width), cosine, sine_table).astype(
        jnp.bfloat16
    )
    values_in = values_in.reshape(length, -1, head_width).astype(jnp.bfloat16)
    upstream = upstream.reshape(length, -1, head_width)
    position = jnp.arange(length, dtype=jnp.int32)
    key_usable = (position >= audio_total) | (position < (frame_count + 1) // 2)
    allowed = (position[None, :] <= position[:, None]) & key_usable[None, :]

    def heads_first(array_in):
        return array_in.transpose(1, 0, 2)

    grad_query, grad_value = lax.map(
        lambda members: decoder_head(members[0], members[1], members[2], members[3], allowed),
        (heads_first(queries), heads_first(keys_in), heads_first(values_in), heads_first(upstream)),
    )
    grad_query = unrotate(heads_first(grad_query), cosine, sine_table).reshape(length, -1)
    grad_value = heads_first(grad_value).reshape(length, -1)
    grads_out = ADAPTER_SCALE * jnp.stack(
        [
            jnp.dot(low_query.T, grad_query, precision=HIGHEST),
            jnp.dot(low_value.T, grad_value, precision=HIGHEST),
        ]
    )
    grads_in = ADAPTER_SCALE * jnp.stack(
        [
            jnp.dot(
                full_rows.T,
                jnp.dot(grad_query, adapter_out[0].T, precision=HIGHEST),
                precision=HIGHEST,
            ),
            jnp.dot(
                full_rows.T,
                jnp.dot(grad_value, adapter_out[1].T, precision=HIGHEST),
                precision=HIGHEST,
            ),
        ]
    )
    return (grads_in, grads_out)


def per_device(
    frames,
    frame_counts,
    encoder_gain,
    encoder_shift,
    encoder_qkv,
    encoder_out,
    post_gain,
    post_shift,
    projector,
    projector_shift,
    text_embed,
    decoder_gain,
    decoder_qkv,
    adapter_in,
    adapter_out,
    audio_upstream,
    text_upstream,
):
    frames_clip = frames[0]
    frame_count = frame_counts[0]
    normed_frames = layer_norm(frames_clip, encoder_gain, encoder_shift).astype(jnp.bfloat16)
    encoder_triple_w, encoder_out_w, projector_rows, decoder_triple_w = (
        lax.all_gather(encoder_qkv, "dp", axis=1, tiled=True),
        lax.all_gather(encoder_out, "dp", axis=1, tiled=True),
        lax.all_gather(projector, "dp", axis=0, tiled=True),
        lax.all_gather(decoder_qkv, "dp", axis=1, tiled=True),
    )
    all_frames = lax.all_gather(normed_frames, "tensor", axis=0, tiled=True)
    triple = jnp.einsum(
        "sd,jdh->jsh", all_frames, encoder_triple_w, preferred_element_type=jnp.float32
    ).astype(jnp.bfloat16)
    position = jnp.arange(all_frames.shape[0], dtype=jnp.int32)
    context = encoder_attention(triple[0], triple[1], triple[2], position < frame_count, EHD)
    partial_terms = jnp.dot(context, encoder_out_w, preferred_element_type=jnp.float32)
    attended = lax.psum_scatter(
        partial_terms.astype(jnp.bfloat16), "tensor", scatter_dimension=0, tiled=True
    ).astype(jnp.float32)
    hidden = frames_clip.astype(jnp.float32) + attended
    pooled = jnp.mean(hidden.reshape(-1, 2, hidden.shape[1]), 1)
    pooled_norm = layer_norm(pooled, post_gain, post_shift).astype(jnp.bfloat16)
    column_count = projector_rows.shape[1]
    pooled_all = lax.all_gather(pooled_norm, "tensor", axis=0, tiled=True)
    shift_part = lax.dynamic_slice_in_dim(
        projector_shift, lax.axis_index("tensor") * column_count, column_count
    )
    half_embed = (
        jnp.dot(pooled_all, projector_rows, preferred_element_type=jnp.float32) + shift_part
    ).astype(jnp.bfloat16)
    embedded = lax.all_to_all(half_embed, "tensor", split_axis=0, concat_axis=1, tiled=True)
    sequence_part = jnp.concatenate([embedded, text_embed[0]], 0)
    normed_part = root_norm(sequence_part, decoder_gain)
    gathered = lax.all_gather(normed_part, "tensor", axis=0, tiled=True)
    audio_rows = embedded.shape[0]
    features = gathered.shape[1]
    blocks = gathered.reshape(lax.axis_size("tensor"), -1, features)
    audio_total = blocks.shape[0] * audio_rows
    normed = jnp.concatenate(
        [
            blocks[:, :audio_rows].reshape(-1, features),
            blocks[:, audio_rows:].reshape(-1, features),
        ],
        0,
    )
    base_triple = jnp.einsum(
        "sd,jdh->jsh", normed, decoder_triple_w, preferred_element_type=jnp.float32
    )
    upstream = jnp.concatenate([audio_upstream[0], text_upstream[0]], 0)
    grads_in, grads_out = adapter_grads(
        normed,
        base_triple[0],
        base_triple[1],
        base_triple[2],
        upstream,
        frame_count,
        audio_total,
        adapter_in,
        adapter_out,
        HD,
    )
    summed_in = lax.psum_scatter(grads_in, ("dp", "tensor"), scatter_dimension=1, tiled=True)
    summed_out = lax.psum_scatter(grads_out, "dp", scatter_dimension=1, tiled=True)
    return (summed_in, summed_out)


def solution(mesh):
    in_specs = (
        P("dp", "tensor", None),
        P("dp"),
        P(),
        P(),
        P(None, "dp", "tensor"),
        P("tensor", "dp"),
        P(),
        P(),
        P("dp", "tensor"),
        P(),
        P("dp", "tensor", None),
        P(),
        P(None, "dp", "tensor"),
        P(),
        P(None, None, "tensor"),
        P("dp", None, "tensor"),
        P("dp", None, "tensor"),
    )
    out_specs = (P(None, ("dp", "tensor"), None), P(None, "dp", "tensor"))
    return jax.shard_map(
        per_device, mesh=mesh, in_specs=in_specs, out_specs=out_specs, check_vma=False
    )
```

profile of v0, /device:TPU:0, one launch (start us, length us, event | category | flops | bytes accessed | tf_op | source)
XLA Modules:
  0.0 917.5 jit_solution(14356626369457512545)
XLA Ops:
  12.8 27.3 %all_gather.23 = bf16[320,1280]{0,1:T(8,128)(2,1)} all-gather(bf16[320,80]{0,1:T(8,128)(2,1)S(1)} %copy-done.20), channel_id=1, replica_groups=mesh['dp'=16,'tensor'=2] {'dp'}, dimensions={1}, use_global_device_ids=true | all-gather | bytes 870400 | tf_op jit(solution)/shard_map/all_gather | solution.py:184
  40.1 27.6 %all-gather.16.cloned.1.call-done = bf16[2,750,1280]{2,1,0:T(8,128)(2,1)} async-done(((bf16[1,750,1280]{2,1,0:T(8,128)(2,1)}), bf16[2,750,1280]{2,1,0:T(8,128)(2,1)}) %all-gather.16.cloned.1.call-update) | async-done | bytes 3840016 | tf_op jit(solution)/shard_map/all_gather | solution.py:188
  67.8 4.7 reshape.167
  72.5 42.4 %all-gather.10.cloned.1.call-done = bf16[3,1280,320]{2,1,0:T(8,128)(2,1)} async-done(((bf16[3,80,320]{2,1,0:T(8,128)(2,1)}), bf16[3,1280,320]{2,1,0:T(8,128)(2,1)}) %all-gather.10.cloned.1.call-update) | async-done | bytes 2457616 | tf_op jit(solution)/shard_map/all_gather | solution.py:183
  114.8 7.0 fusion.86
  130.4 41.4 %while.24 = (s32[]{:T(128)}, bf16[5,1500,64]{1,2,0:T(8,128)(2,1)}, bf16[5,1500,64]{2,1,0:T(8,128)(2,1)}, bf16[5,1500,64]{2,1,0:T(8,128)(2,1)}, bf16[5,1500,64]{2,1,0:T(8,128)(2,1)}, /*index=5*/s32[]{:T(128)}, s32[]{:T(128)}) while((s32[]{:T(128)}, bf16[5,1500,64]{1,2,0:T(8,128)(2,1)}, bf16[5,1500,64]{2,1,0:T(8,128)(2,1)}, ...), condition=%wide.region_5.6_spmd.clone, body=%wide.region_2.5_spmd.clone.sunk | while | flops 594094464 | bytes 28386808 | solution.py:50
  171.9 5.3 convolution_convert_fusion.1
  177.2 50.5 %fusion.4 = bf16[752,1280]{1,0:T(8,128)(2,1)} fusion(bf16[1500,1280]{1,0:T(8,128)(2,1)} %convolution_convert_fusion.1), kind=kCustom, calls=%all-reduce-scatter | all-reduce-scatter fusion | flops 1925121 | bytes 5765632
  232.3 12.4 %concatenate.43 = bf16[754,1280]{1,0:T(8,128)(2,1)} concatenate(bf16[2,1280]{1,0:T(2,128)(2,1)S(1)} %collective-permute-done, bf16[752,1280]{1,0:T(8,128)(2,1)} %fusion.4), dimensions={0} | concatenate | bytes 3860480
  244.6 4.0 fusion.57
  248.6 5.5 reshape.153
  254.1 6.7 reduce_sum.83
  263.5 29.8 %all-gather.18.cloned.1.call-done = bf16[2,375,1280]{2,1,0:T(8,128)(2,1)} async-done(((bf16[1,375,1280]{2,1,0:T(8,128)(2,1)}), bf16[2,375,1280]{2,1,0:T(8,128)(2,1)}) %all-gather.18.cloned.1.call-update) | async-done | bytes 1920016 | tf_op jit(solution)/shard_map/all_gather | solution.py:202
  295.2 43.5 %all-gather.12.cloned.1.call-done = bf16[1280,1024]{1,0:T(8,128)(2,1)} async-done(((bf16[80,1024]{1,0:T(8,128)(2,1)}), bf16[1280,1024]{1,0:T(8,128)(2,1)}) %all-gather.12.cloned.1.call-update) | async-done | bytes 2621456 | tf_op jit(solution)/shard_map/all_gather | solution.py:185
  338.7 3.9 add_convert_fusion
  344.1 3.7 all-to-all-start
  349.0 18.2 %all-to-all-done = bf16[2,375,1024]{2,1,0:T(8,128)(2,1)S(1)} async-done(((bf16[2,375,1024]{2,1,0:T(8,128)(2,1)}), bf16[2,375,1024]{2,1,0:T(8,128)(2,1)S(1)}, u32[]{:S(2)}, u32[]{:S(2)}) %all-to-all-start) | async-done | bytes 1536032 | tf_op jit(solution)/shard_map/all_to_all | solution.py:209
  373.5 3.9 copy.56
  386.8 35.1 %all-gather.20.cloned.1.call-done = bf16[2,396,2048]{2,1,0:T(8,128)(2,1)} async-done(((bf16[1,396,2048]{2,1,0:T(8,128)(2,1)}), bf16[2,396,2048]{2,1,0:T(8,128)(2,1)}) %all-gather.20.cloned.1.call-update) | async-done | bytes 3244048 | tf_op jit(solution)/shard_map/all_gather | solution.py:212
  429.5 6.2 fusion.103
  435.7 3.8 fusion.105
  439.5 85.1 %all-gather.14.cloned.1.call-done = bf16[3,2048,1024]{2,1,0:T(8,128)(2,1)} async-done(((bf16[3,128,1024]{2,1,0:T(8,128)(2,1)}), bf16[3,2048,1024]{2,1,0:T(8,128)(2,1)}) %all-gather.14.cloned.1.call-update) | async-done | bytes 12582928 | tf_op jit(solution)/shard_map/all_gather | solution.py:186
  524.7 13.2 %convolution_bitcast_fusion.1 = f32[3,792,1024]{2,1,0:T(8,128)S(1)} fusion(bf16[3,2048,1024]{2,1,0:T(8,128)(2,1)} %all-gather.14.cloned.1.call-done, bf16[42,2048]{1,0:T(8,128)(2,1)} %reshape.156, bf16[750,2048]{1,0:T(8,128)(2,1)S(1)} %copy-done.7), kind=kOutput, calls=%fused_computation.75 | convolution fusion | flops 9972154368 | bytes 25559040 | tf_op jit(solution)/shard_map/sd,jdh->jsh/dot_general | solution.py:224
  551.5 11.3 %slice_negate_fusion.1 = (f32[792,8,64]{2,0,1:T(8,128)}, f32[792,8,64]{2,0,1:T(8,128)}, f32[792,8,64]{2,0,1:T(8,128)}, f32[792,8,64]{2,0,1:T(8,128)}) fusion(f32[792,8,128]{2,0,1:T(8,128)} %copy.60, f32[792,8,128]{2,0,1:T(8,128)} %bitcast.248), kind=kLoop, calls=%fused_computation.89 | loop fusion | flops 811008 | bytes 12976128 | tf_op jit(solution)/shard_map/neg | solution.py:67
  562.8 8.4 fusion.93
  571.2 94.6 %while.25 = (s32[]{:T(128)}, f32[8,792,128]{2,1,0:T(8,128)}, f32[8,792,128]{2,1,0:T(8,128)}, bf16[8,792,128]{2,1,0:T(8,128)(2,1)}, bf16[8,792,128]{2,1,0:T(8,128...) while((s32[]{:T(128)}, f32[8,792,128]{2,1,0:T(8,128)}, ...), condition=%wide.region_15.16_spmd.clone, body=%wide.region_11.15_spmd.clone.sunk | while | flops 813438592 | bytes 21450224 | solution.py:131
  576.8 3.6 fusion.173
  612.1 3.6 fusion.173
  647.6 3.6 fusion.173
  659.4 3.6 fusion.173
  692.8 78.6 %all-reduce.5.cloned.1.call-done = f32[2,64,1024]{2,1,0:T(8,128)} async-done(((f32[2,64,1024]{2,1,0:T(8,128)}), f32[2,64,1024]{2,1,0:T(8,128)}) %all-reduce.5.cloned.1.call-update) | async-done | bytes 524304
  772.9 136.1 %reduce-scatter.7.cloned.1.call-done = f32[64,128]{1,0:T(8,128)} async-done(((f32[2048,128]{1,0:T(8,128)}), f32[64,128]{1,0:T(8,128)}) %reduce-scatter.7.cloned.1.call-update) | async-done | bytes 32784
  (220 shorter events, 211.6 us)
Async XLA Ops:
  7.2 2.1 copy-start.1
  7.2 2.8 copy-start.22
  7.2 2.8 copy-start.21
  7.2 60.6 %all-gather.16.cloned.1.call-start = ((), (), s32[]{:S(2)}) async-start(), calls=%async_computation.5 | async-start | bytes 5775360 | tf_op jit(solution)/shard_map/all_gather | solution.py:188
  9.9 2.9 copy-start.20
  12.0 102.8 %all-gather.10.cloned.1.call-start = ((), (), s32[]{:S(2)}) async-start(), calls=%async_computation.2 | async-start | bytes 3133440 | tf_op jit(solution)/shard_map/all_gather | solution.py:183
  12.8 280.5 %all-gather.18.cloned.1.call-start = ((), (), s32[]{:S(2)}) async-start(), calls=%async_computation.6 | async-start | bytes 2887680 | tf_op jit(solution)/shard_map/all_gather | solution.py:202
  130.4 41.4 %copy-start.12 = (bf16[320,1280]{0,1:T(8,128)(2,1)S(1)}, bf16[320,1280]{0,1:T(8,128)(2,1)}, u32[]{:S(2)}) copy-start(bf16[320,1280]{0,1:T(8,128)(2,1)} %all_gather.23) | copy-start | bytes 2457604
  177.2 53.7 %copy-start.26 = (u32[32]{0:T(128)S(1)}, u32[32]{0:T(128)}, u32[]{:S(2)}) copy-start(u32[32]{0:T(128)} %constant.103) | copy-start | bytes 388
  228.5 3.8 collective-permute-start
  262.9 75.8 %all-gather.12.cloned.1.call-start = ((), (), s32[]{:S(2)}) async-start(), calls=%async_computation.3 | async-start | bytes 2785280 | tf_op jit(solution)/shard_map/all_gather | solution.py:185
  263.5 75.2 %dynamic-slice-start = ((f32[2048]{0:T(1024)}, s32[]{:T(128)}), f32[1024]{0:T(1024)S(1)}, s32[]{:S(2)}) async-start(f32[2048]{0:T(1024)} %param.30, s32[]{:T(128)} %select_n.16), calls=%async_computation.11 | async-start | bytes 8704 | tf_op jit(solution)/shard_map/dynamic_slice | solution.py:203
  342.6 5.4 copy-start.18
  344.1 23.2 %all-to-all-start = ((bf16[2,375,1024]{2,1,0:T(8,128)(2,1)}), bf16[2,375,1024]{2,1,0:T(8,128)(2,1)S(1)}, u32[]{:S(2)}, u32[]{:S(2)}) async-start(bf16[2,375,1024]{2,1,0:T(8,128)(2,1)} %all_to_all.14), calls=%async_computation | async-start | bytes 3080192 | tf_op jit(solution)/shard_map/all_to_all | solution.py:209
  347.7 22.3 %copy-start.25 = (f32[2048]{0:T(1024)S(1)}, f32[2048]{0:T(1024)}, u32[]{:S(2)}) copy-start(f32[2048]{0:T(1024)} %param.32) | copy-start | bytes 24580
  347.8 74.1 %all-gather.20.cloned.1.call-start = ((), (), s32[]{:S(2)}) async-start(), calls=%async_computation.7 | async-start | bytes 4915200 | tf_op jit(solution)/shard_map/all_gather | solution.py:212
  373.5 5.3 copy-start.11
  377.5 2.1 copy-start.19
  377.5 147.2 %all-gather.14.cloned.1.call-start = ((), (), s32[]{:S(2)}) async-start(), calls=%async_computation.4 | async-start | bytes 13369344 | tf_op jit(solution)/shard_map/all_gather | solution.py:186
  378.1 393.3 %all-reduce.5.cloned.1.call-start = ((), (), s32[]{:S(2)}) async-start(), calls=%async_computation.9 | async-start | bytes 1048576
  426.0 9.7 %copy-start.7 = (bf16[750,2048]{1,0:T(8,128)(2,1)S(1)}, bf16[750,2048]{1,0:T(8,128)(2,1)}, u32[]{:S(2)}) copy-start(bf16[750,2048]{1,0:T(8,128)(2,1)} %reshape.155) | copy-start | bytes 9216004
  429.5 6.2 copy-start.16
  429.5 6.2 copy-start.27
  539.0 4.4 copy-start.14
  546.4 2.8 copy-start.2
  551.5 11.4 %copy-start.5 = (f32[792,128]{1,0:T(8,128)S(1)}, f32[792,128]{1,0:T(8,128)}, u32[]{:S(2)}) copy-start(f32[792,128]{1,0:T(8,128)} %get-tuple-element.179) | copy-start | bytes 1216516
  669.9 3.2 copy-start.10
  670.9 5.6 copy-start.3
  678.8 4.5 copy-start.8
  683.0 226.0 %reduce-scatter.7.cloned.1.call-start = ((), (), s32[]{:S(2)}) async-start(), calls=%async_computation.8 | async-start | bytes 1081344
  683.2 3.0 copy-start.17
  688.3 3.2 copy-start.28
  (16 other events, 19.2 us)
Sparse Core Ops, SparseCore 0:
  12.1 55.5 all-gather.15
  69.9 44.8 all-gather.9
  263.0 30.2 all-gather.17
  295.5 43.1 all-gather.11
  377.6 44.1 all-gather.19
  423.9 100.7 all-gather.13
  683.1 88.2 all-reduce.4
  773.6 135.2 reduce-scatter.6
where the time goes:
time: 930 us; the launch traced here: 917 us
  waiting for transfers between devices  498 us (54%)
  matrix products  171 us (18%)
  blocking collectives  77.8 us (8%)
  local copies, waits for them, and re-layouts  77.6 us (8%)
  other arithmetic  68.7 us (7%)
  between operations  16.9 us (2%)
    unnamed x11, waiting for transfers between devices  217 us
    all_gather x1, waiting for transfers between devices, per_device(): lax.all_gather(decoder_qkv, 'dp', axis=1, tiled=True)  85.1 us
    unnamed x1, blocking collectives  50.5 us
    all_gather x1, waiting for transfers between devices, per_device(): lax.all_gather(projector, 'dp', axis=0, tiled=True)  43.5 us
    all_gather x1, waiting for transfers between devices, per_device(): lax.all_gather(encoder_qkv, 'dp', axis=1, tiled=True)  42.4 us
    unnamed x73, local copies, waits for them, and re-layouts  38 us
    all_gather x1, waiting for transfers between devices, per_device(): gathered = lax.all_gather(normed_part, 'tensor', axis=0, tiled=True)  35.1 us
    all_gather x1, waiting for transfers between devices, per_device(): pooled_all = lax.all_gather(pooled_norm, 'tensor', axis=0, tiled=True)  29.8 us
  transfers between devices with their start and end apart: 10, of which 10 were waited for; matrix products, arithmetic and copies ran while one was open for 5% of the time, Pallas kernels for 0%

commit v1 on v0

v1 whole, which is shorter than its diff:
```python
import functools

import jax
import jax.numpy as jnp
from jax import lax
from jax.experimental import pallas as pl
from jax.experimental.pallas import tpu as pltpu
from jax.sharding import PartitionSpec as P

EHD = 64
HD = 128
RANK = 64

EPS_LAYER = 1e-05
EPS_ROOT = 1e-06
ADAPTER_SCALE = 2.0
ROPE_BASE = 10000.0
LOG2E = 1.4426950408889634
VMEM_BYTES = 56 * 1024 * 1024
F32 = jnp.float32
BF16 = jnp.bfloat16
MESH = pl.DeviceIdType.MESH


def round_up(value, unit):
    return -(-value // unit) * unit


def dot(a, b):
    return jnp.dot(a, b, preferred_element_type=F32)


def dot_t(a, b):
    return lax.dot_general(a, b, (((1,), (1,)), ((), ())), preferred_element_type=F32)


def dot_0(a, b):
    return lax.dot_general(a, b, (((0,), (0,)), ((), ())), preferred_element_type=F32)


def params():
    return pltpu.CompilerParams(vmem_limit_bytes=VMEM_BYTES)


def layer_norm(values, gain, shift):
    center = values - jnp.mean(values, -1, keepdims=True)
    spread = jnp.mean(center * center, -1, keepdims=True)
    return center * lax.rsqrt(spread + EPS_LAYER) * gain + shift


def pair_matrix(rows):
    row = lax.broadcasted_iota(jnp.int32, (rows // 2, rows), 0)
    col = lax.broadcasted_iota(jnp.int32, (rows // 2, rows), 1)
    return jnp.where((col == 2 * row) | (col == 2 * row + 1), 0.5, 0.0).astype(BF16)


def encode_kernel(length, frames, gain, shift, weights, triple, pooled):
    tile, width = frames.shape
    base = pl.program_id(0) * tile
    index = lax.broadcasted_iota(jnp.int32, (tile, 1), 0) + base
    rows = jnp.where(index < length, frames[...].astype(F32), 0.0)
    pooled[...] = dot(pair_matrix(tile), rows.astype(BF16))
    normed = layer_norm(rows, gain[...], shift[...]).astype(BF16)
    for j in range(3):
        triple[j] = dot(normed, weights[:, j].reshape(width, -1)).astype(BF16)


def encode(frames, gain, shift, weights):
    length, width = frames.shape
    parts, _, depth, columns = weights.shape
    tile = 256
    padded = round_up(length, 2 * tile)
    whole = lambda shape: pl.BlockSpec(shape, lambda i: (0,) * len(shape))
    return pl.pallas_call(
        functools.partial(encode_kernel, length),
        grid=(padded // tile,),
        in_specs=[
            pl.BlockSpec((tile, width), lambda i: (i, 0)),
            whole((1, width)),
            whole((1, width)),
            whole((parts, 3, depth, columns)),
        ],
        out_specs=[
            pl.BlockSpec((3, tile, columns), lambda i: (0, i, 0)),
            pl.BlockSpec((tile // 2, width), lambda i: (i, 0)),
        ],
        out_shape=[
            jax.ShapeDtypeStruct((3, padded, columns), BF16),
            jax.ShapeDtypeStruct((padded // 2, width), F32),
        ],
        compiler_params=params(),
        cost_estimate=pl.CostEstimate(
            flops=6 * padded * width * columns, bytes_accessed=14 * 2**20, transcendentals=0
        ),
        name="encode",
    )(frames, gain[None], shift[None], weights)


def encoder_attention_kernel(count, queries, keys, values, out):
    tile, columns = queries.shape[1:]
    total = keys.shape[1]
    index = lax.broadcasted_iota(jnp.int32, (1, total), 1)
    bias = jnp.where(index < count[0], 0.0, -jnp.inf)
    pairs = pair_matrix(tile)
    for head in range(columns // EHD):
        span = slice(head * EHD, (head + 1) * EHD)
        scores = dot_t(queries[0, :, span], keys[0, :, span]) * (EHD**-0.5 * LOG2E) + bias
        weights = jnp.exp2(scores - jnp.max(scores, -1, keepdims=True))
        total_weight = jnp.sum(weights, -1, keepdims=True)
        context = dot(weights.astype(BF16), values[0, :, span]) / total_weight
        out[:, span] = dot(pairs, context.astype(BF16)).astype(BF16)


def encoder_attention(triple, count):
    _, padded, columns = triple.shape
    tile = 512
    return pl.pallas_call(
        encoder_attention_kernel,
        grid=(padded // tile,),
        in_specs=[
            pl.BlockSpec(memory_space=pltpu.SMEM),
            pl.BlockSpec((1, tile, columns), lambda i: (0, i, 0)),
            pl.BlockSpec((1, padded, columns), lambda i: (1, 0, 0)),
            pl.BlockSpec((1, padded, columns), lambda i: (2, 0, 0)),
        ],
        out_specs=pl.BlockSpec((tile // 2, columns), lambda i: (i, 0)),
        out_shape=jax.ShapeDtypeStruct((padded // 2, columns), BF16),
        compiler_params=params(),
        cost_estimate=pl.CostEstimate(
            flops=16 * padded * padded * columns,
            bytes_accessed=4 * 2**20,
            transcendentals=padded * padded * (columns // EHD),
        ),
        name="encoder_attention",
    )(count, triple, triple, triple)


def embed_kernel(
    audio, pooled, context_a, context_b, out_w, gain, shift, proj_a, proj_b, proj_shift,
    text, root_gain, low_w, normed_out, low_out,
):
    tile = pooled.shape[0]
    half = out_w.shape[0] // 2
    hidden = pooled[...] + dot(context_a[...], out_w[:half]) + dot(context_b[...], out_w[half:])
    pooled_norm = layer_norm(hidden, gain[...], shift[...]).astype(BF16)
    columns = proj_a.shape[1]
    first = (dot(pooled_norm, proj_a[...]) + proj_shift[:, :columns]).astype(BF16)
    second = (dot(pooled_norm, proj_b[...]) + proj_shift[:, columns:]).astype(BF16)
    embedded = jnp.concatenate([first, second], 1).astype(F32)
    index = lax.broadcasted_iota(jnp.int32, (tile, 1), 0) + pl.program_id(0) * tile
    rows = jnp.where(index < audio, embedded, text[...].astype(F32))
    scale = lax.rsqrt(jnp.mean(rows * rows, -1, keepdims=True) + EPS_ROOT)
    normed = (rows * scale * root_gain[...]).astype(BF16)
    normed_out[...] = normed
    low_out[...] = dot(normed, low_w[...]).astype(BF16)


def embed(audio, pooled, context_a, context_b, out_w, gain, shift, proj_a, proj_b, proj_shift,
          text, root_gain, low_w):
    total, features = text.shape
    width = pooled.shape[1]
    tile = 128
    last = pooled.shape[0] // tile - 1
    whole = lambda shape: pl.BlockSpec(shape, lambda i: (0,) * len(shape))
    held = lambda i: (jnp.minimum(i, last), 0)
    row = lambda i: (i, 0)
    return pl.pallas_call(
        functools.partial(embed_kernel, audio),
        grid=(total // tile,),
        in_specs=[
            pl.BlockSpec((tile, width), held),
            pl.BlockSpec((tile, context_a.shape[1]), held),
            pl.BlockSpec((tile, context_b.shape[1]), held),
            whole(out_w.shape),
            whole((1, width)),
            whole((1, width)),
            whole(proj_a.shape),
            whole(proj_b.shape),
            whole((1, features)),
            pl.BlockSpec((tile, features), row),
            whole((1, features)),
            whole(low_w.shape),
        ],
        out_specs=[
            pl.BlockSpec((tile, features), row),
            pl.BlockSpec((tile, low_w.shape[1]), row),
        ],
        out_shape=[
            jax.ShapeDtypeStruct((total, features), BF16),
            jax.ShapeDtypeStruct((total, low_w.shape[1]), BF16),
        ],
        compiler_params=params(),
        cost_estimate=pl.CostEstimate(
            flops=2 * total * width * features * 2, bytes_accessed=24 * 2**20, transcendentals=0
        ),
        name="embed",
    )(pooled, context_a, context_b, out_w, gain[None], shift[None], proj_a, proj_b,
      proj_shift[None], text, root_gain[None], low_w)


def decoder_kernel(
    audio, count, normed, low, weights, up_w, upstream, cosine, sine, grads_out, grads_in,
    terms, grad_value,
):
    total, features = normed.shape
    step = pl.program_id(0)
    depth = weights.shape[1] // 3
    columns = weights.shape[2]
    scale = HD**-0.5

    @pl.when(step == 0)
    def _():
        terms[...] = jnp.zeros_like(terms)

    rows = normed[...]
    base = [
        dot(rows, weights[:, j * depth:(j + 1) * depth].reshape(features, columns))
        for j in range(3)
    ]
    up_q = up_w[0].astype(BF16)
    up_v = up_w[1].astype(BF16)
    low_q = low[:, :RANK]
    low_v = low[:, RANK:]
    all_q = base[0] + ADAPTER_SCALE * dot(low_q, up_q)
    all_v = (base[2] + ADAPTER_SCALE * dot(low_v, up_v)).astype(BF16)
    cos_t = cosine[...]
    sin_t = sine[...]
    usable = (count[0] + 1) // 2
    block = 256
    for head in range(columns // HD):
        span = slice(head * HD, (head + 1) * HD)
        q = all_q[:, span]
        k = base[1][:, span]
        q = (q * cos_t + pltpu.roll(q, HD // 2, 1) * sin_t).astype(BF16)
        k = (k * cos_t + pltpu.roll(k, HD // 2, 1) * sin_t).astype(BF16)
        v = all_v[:, span]
        u = upstream[:, span]
        grad_value[...] = jnp.zeros_like(grad_value)
        pieces = []
        for start in range(0, total, block):
            stop = min(start + block, total)
            key = lax.broadcasted_iota(jnp.int32, (stop - start, stop), 1)
            query = lax.broadcasted_iota(jnp.int32, (stop - start, stop), 0) + start
            allowed = (key <= query) & ((key >= audio) | (key < usable))
            scores = dot_t(q[start:stop], k[:stop]) * (scale * LOG2E)
            scores = jnp.where(allowed, scores, -jnp.inf)
            w = jnp.exp2(scores - jnp.max(scores, -1, keepdims=True))
            over = 1.0 / jnp.sum(w, -1, keepdims=True)
            w16 = w.astype(BF16)
            context = (dot(w16, v[:stop]) * over).astype(BF16)
            ub = u[start:stop].astype(F32)
            delta = jnp.sum(ub * context.astype(F32), -1, keepdims=True) * over
            scaled = (ub * over).astype(BF16)
            grad_probs = dot_t(scaled, v[:stop])
            dscores = (w * (grad_probs - delta)).astype(BF16)
            pieces.append(dot(dscores, k[:stop]) * scale)
            grad_value[:stop] += dot_0(w16, scaled)
        gq = jnp.concatenate(pieces, 0)
        gq = (gq * cos_t - pltpu.roll(gq, HD // 2, 1) * sin_t).astype(BF16)
        gv = grad_value[...].astype(BF16)
        grads_out[0, :, span] = ADAPTER_SCALE * dot_0(low_q, gq)
        grads_out[1, :, span] = ADAPTER_SCALE * dot_0(low_v, gv)
        terms[:, :RANK] += dot_t(gq, up_q[:, span])
        terms[:, RANK:] += dot_t(gv, up_v[:, span])

    @pl.when(step == pl.num_programs(0) - 1)
    def _():
        grads_in[...] = ADAPTER_SCALE * dot_0(terms[...].astype(BF16), rows)


def decoder(audio, count, normed, low, weights, up_w, upstream, cosine, sine):
    total, features = normed.shape
    parts, deep, all_columns = weights.shape
    columns = 2 * HD
    whole = lambda shape: pl.BlockSpec(shape, lambda i: (0,) * len(shape))
    return pl.pallas_call(
        functools.partial(decoder_kernel, audio),
        grid=(all_columns // columns,),
        in_specs=[
            pl.BlockSpec(memory_space=pltpu.SMEM),
            whole((total, features)),
            whole((total, 2 * RANK)),
            pl.BlockSpec((parts, deep, columns), lambda i: (0, 0, i)),
            pl.BlockSpec((2, RANK, columns), lambda i: (0, 0, i)),
            pl.BlockSpec((total, columns), lambda i: (0, i)),
            whole((total, HD)),
            whole((total, HD)),
        ],
        out_specs=[
            pl.BlockSpec((2, RANK, columns), lambda i: (0, 0, i)),
            whole((2 * RANK, features)),
        ],
        out_shape=[
            jax.ShapeDtypeStruct((2, RANK, all_columns), F32),
            jax.ShapeDtypeStruct((2 * RANK, features), F32),
        ],
        scratch_shapes=[pltpu.VMEM((total, 2 * RANK), F32), pltpu.VMEM((total, HD), F32)],
        compiler_params=params(),
        cost_estimate=pl.CostEstimate(
            flops=2 * total * features * all_columns * 5,
            bytes_accessed=24 * 2**20,
            transcendentals=total * total * 8,
        ),
        name="decoder",
    )(count, normed, low, weights, up_w, upstream, cosine, sine)


def reduce_kernel(parts, shared, terms, out, landed, mine, theirs, send_sem, recv_sem, pair_sem):
    dp = lax.axis_index("dp")
    tensor = lax.axis_index("tensor")
    partner = (dp, 1 - tensor)
    barrier = pltpu.get_barrier_semaphore()
    for k in range(1, parts):
        pl.semaphore_signal(
            barrier, inc=1, device_id=(lax.rem(dp + k, parts), tensor), device_id_type=MESH
        )
    pl.semaphore_signal(barrier, inc=1, device_id=partner, device_id_type=MESH)
    pl.semaphore_wait(barrier, parts)
    copies = []
    for k in range(1, parts):
        peer = lax.rem(dp + k, parts)
        copy = pltpu.make_async_remote_copy(
            src_ref=terms.at[peer],
            dst_ref=landed.at[k - 1],
            send_sem=send_sem.at[k - 1],
            recv_sem=recv_sem.at[k - 1],
            device_id=(peer, tensor),
            device_id_type=MESH,
        )
        copy.start()
        copies.append(copy)
    total = terms[dp].astype(F32)
    for k, copy in enumerate(copies):
        copy.wait()
        total = total + landed[k].astype(F32)
    mine[...] = total[:shared]
    copy = pltpu.make_async_remote_copy(
        src_ref=mine, dst_ref=theirs, send_sem=pair_sem.at[0], recv_sem=pair_sem.at[1],
        device_id=partner, device_id_type=MESH,
    )
    copy.start()
    out[shared:] = total[shared:]
    copy.wait()
    out[:shared] = total[:shared] + theirs[...]


def reduce_terms(terms, shared):
    parts, rows, columns = terms.shape
    return pl.pallas_call(
        functools.partial(reduce_kernel, parts, shared),
        out_shape=jax.ShapeDtypeStruct((rows, columns), F32),
        in_specs=[pl.BlockSpec(memory_space=pltpu.VMEM)],
        out_specs=pl.BlockSpec(memory_space=pltpu.VMEM),
        scratch_shapes=[
            pltpu.VMEM((parts - 1, rows, columns), BF16),
            pltpu.VMEM((shared, columns), F32),
            pltpu.VMEM((shared, columns), F32),
            pltpu.SemaphoreType.DMA((parts - 1,)),
            pltpu.SemaphoreType.DMA((parts - 1,)),
            pltpu.SemaphoreType.DMA((2,)),
        ],
        compiler_params=pltpu.CompilerParams(
            collective_id=0, has_side_effects=True, vmem_limit_bytes=VMEM_BYTES
        ),
        name="reduce_terms",
    )(terms)


def rope_tables(length):
    position = jnp.arange(length).astype(F32)
    frequency = ROPE_BASE ** (-jnp.arange(0, HD, 2).astype(F32) / HD)
    angles = position[:, None] * frequency[None, :]
    cosine, sine = jnp.cos(angles), jnp.sin(angles)
    return jnp.concatenate([cosine, cosine], -1), jnp.concatenate([-sine, sine], -1)


def both(value, axis):
    other = lax.ppermute(value, "tensor", [(0, 1), (1, 0)])
    first = lax.axis_index("tensor") == 0
    return jnp.where(first, value, other), jnp.where(first, other, value)


def per_device(
    frames,
    frame_counts,
    encoder_gain,
    encoder_shift,
    encoder_qkv,
    encoder_out,
    post_gain,
    post_shift,
    projector,
    projector_shift,
    text_embed,
    decoder_gain,
    decoder_qkv,
    adapter_in,
    adapter_out,
    audio_upstream,
    text_upstream,
):
    parts = lax.axis_size("dp")
    encoder_w = lax.all_gather(encoder_qkv, "dp")
    audio, columns = audio_upstream.shape[1:]
    text_rows = text_upstream.shape[1]
    total = round_up(audio + text_rows, 128)
    tail = total - audio - text_rows

    all_frames = jnp.concatenate(both(frames[0], 0), 0)
    text = jnp.concatenate(both(text_embed[0], 0), 0)
    text = jnp.pad(text, ((audio, tail), (0, 0)))
    upstream = jnp.pad(
        jnp.concatenate([audio_upstream[0], text_upstream[0]], 0), ((0, tail), (0, 0))
    )
    deep = decoder_qkv.shape[1]
    flat = encoder_out.reshape(-1)
    flat = jnp.pad(flat, (0, round_up(flat.size, columns) - flat.size))
    late = jnp.concatenate([flat.reshape(-1, columns), projector], 0)
    encoder_w, late = lax.optimization_barrier((encoder_w, late))
    if encoder_w.shape[2] % 16:
        encoder_w = encoder_w.transpose(1, 0, 2, 3).reshape(1, 3, -1, encoder_w.shape[3])
    late = lax.all_gather(late, "dp")
    split = late.shape[1] - projector.shape[0]
    late, decoder_rows = lax.optimization_barrier(
        (late, decoder_qkv.reshape(3 * deep, columns))
    )
    decoder_w = lax.all_gather(decoder_rows, "dp")
    out_half = late[:, :split].reshape(parts, -1)[:, :encoder_out.size]
    out_half = out_half.reshape((parts,) + encoder_out.shape).transpose(1, 0, 2)
    out_w = jnp.concatenate(both(out_half.reshape(encoder_out.shape[0], -1), 0), 0)
    proj_a, proj_b = both(late[:, split:].reshape(-1, columns), 1)

    triple, pooled = encode(all_frames, encoder_gain, encoder_shift, encoder_w)
    context = encoder_attention(triple, frame_counts)
    context_a, context_b = both(context, 1)
    low_w = jnp.concatenate([adapter_in[0], adapter_in[1]], 1).astype(BF16)
    normed, low = embed(
        audio, pooled, context_a, context_b, out_w, post_gain, post_shift, proj_a, proj_b,
        projector_shift, text, decoder_gain, low_w,
    )
    cosine, sine = rope_tables(total)
    grads_out, grads_in = decoder(
        audio, frame_counts, normed, low, decoder_w, adapter_out, upstream, cosine, sine
    )
    share = grads_in.shape[1] // parts
    ranks = RANK // parts if RANK >= parts else 1
    packed_in = grads_in.reshape(2 * RANK, parts, share).transpose(1, 0, 2)
    packed_out = grads_out.reshape(2, parts, ranks, columns).transpose(1, 0, 2, 3)
    shared = 2 * RANK
    packed = jnp.concatenate(
        [packed_in.astype(BF16), packed_out.astype(BF16).reshape(parts, -1, share)], 1
    )
    summed = reduce_terms(packed, shared)
    half = share // lax.axis_size("tensor")
    part_in = lax.dynamic_slice_in_dim(summed[:shared], lax.axis_index("tensor") * half, half, 1)
    part_in = part_in.reshape(2, RANK, half).transpose(0, 2, 1)
    part_out = summed[shared:].reshape(2, ranks, columns)
    return (part_in, part_out)


def solution(mesh):
    in_specs = (
        P("dp", "tensor", None),
        P("dp"),
        P(),
        P(),
        P(None, "dp", "tensor"),
        P("tensor", "dp"),
        P(),
        P(),
        P("dp", "tensor"),
        P(),
        P("dp", "tensor", None),
        P(),
        P(None, "dp", "tensor"),
        P(),
        P(None, None, "tensor"),
        P("dp", None, "tensor"),
        P("dp", None, "tensor"),
    )
    out_specs = (P(None, ("dp", "tensor"), None), P(None, "dp", "tensor"))
    return jax.shard_map(
        per_device, mesh=mesh, in_specs=in_specs, out_specs=out_specs, check_vma=False
    )
```

time: 930 us -> 365 us (0.39); the launches traced: 917 us -> 362 us
  waiting for transfers between devices: 498 us -> 155 us
  matrix products: 171 us -> 0 us
  Pallas kernels: 0 us -> 136 us
  blocking collectives: 77.8 us -> 0 us
  local copies, waits for them, and re-layouts: 77.6 us -> 26.4 us
  other arithmetic: 68.7 us -> 24.7 us
    unnamed x11 -> x3, waiting for transfers between devices: 217 us -> 0.71 us
    dot_general x56 -> x0, matrix products: 171 us -> none  [the longest x8 28.7 us: decoder_head(): jnp.dot(grad_scores, keys_in, preferred_element_type=jnp.float32)]
    all_gather x6 -> x3, waiting for transfers between devices: 264 us -> 95.1 us  [the longest x1 48.1 us: per_device(): late = lax.all_gather(late, 'dp')]
    pallas_call x0 -> x5, Pallas kernels: none -> 136 us  [the longest x1 47.3 us: decoder(): pl.pallas_call(functools.partial(decoder_kernel, audio), grid=(all_column...]
    ppermute x0 -> x5, waiting for transfers between devices: none -> 58.8 us  [both(): other = lax.ppermute(value, 'tensor', [(0, 1), (1, 0)])]
    unnamed x1 -> x0, blocking collectives: 50.5 us -> none
    unnamed x73 -> x19, local copies, waits for them, and re-layouts: 38 us -> 3.36 us
    all_gather x1 -> x0, blocking collectives: 27.3 us -> none  [per_device(): lax.all_gather(encoder_out, 'dp', axis=1, tiled=True)]
  transfers between devices with their start and end apart: 10 -> 8, of which waited for: 10 -> 5; matrix products, arithmetic and copies ran while one was open for 5% -> 12% of each run, Pallas kernels for 0% -> 18%
where the time goes in v1:
time: 365 us; the launch traced here: 362 us
  waiting for transfers between devices  155 us (42%)
  Pallas kernels  136 us (37%)
  local copies, waits for them, and re-layouts  26.4 us (7%)
  other arithmetic  24.7 us (7%)
  between operations  14.6 us (4%)
  starting transfers between devices  5.83 us (2%)
    ppermute x5, waiting for transfers between devices, both(): other = lax.ppermute(value, 'tensor', [(0, 1), (1, 0)])  58.8 us
    all_gather x1, waiting for transfers between devices, per_device(): late = lax.all_gather(late, 'dp')  48.1 us
    pallas_call x1, Pallas kernels, decoder(): pl.pallas_call(functools.partial(decoder_kernel, audio), grid=(all_column...  47.3 us
    all_gather x1, waiting for transfers between devices, per_device(): encoder_w = lax.all_gather(encoder_qkv, 'dp')  47 us
    pallas_call x1, Pallas kernels, encoder_attention(): pl.pallas_call(encoder_attention_kernel, grid=(padded // tile,), in_specs...  34.6 us
    pallas_call x1, Pallas kernels, reduce_terms(): pl.pallas_call(functools.partial(reduce_kernel, parts, shared), out_shape...  22.3 us
    pallas_call x1, Pallas kernels, embed(): pl.pallas_call(functools.partial(embed_kernel, audio), grid=(total // til...  18.7 us
    pallas_call x1, Pallas kernels, encode(): pl.pallas_call(functools.partial(encode_kernel, length), grid=(padded //...  13.1 us
  transfers between devices with their start and end apart: 8, of which 5 were waited for; matrix products, arithmetic and copies ran while one was open for 12% of the time, Pallas kernels for 18%

profile of v1, /device:TPU:0, one launch (start us, length us, event | category | flops | bytes accessed | tf_op | source)
XLA Modules:
  0.0 362.0 jit_solution(16188614412371534416)
XLA Ops:
  9.1 1.7 pad_maximum_fusion.6
  10.8 47.0 %all-gather.8.cloned.1.call-done = bf16[48,80,320]{2,1,0:T(8,128)(2,1)} async-done(((bf16[3,80,320]{2,1,0:T(8,128)(2,1)}), bf16[48,80,320]{2,1,0:T(8,128)(2,1)}) %all-gather.8.cloned.1.call-update) | async-done | bytes 2457616 | tf_op jit(solution)/shard_map/all_gather | solution.py:403
  57.8 48.1 %all-gather.12.cloned.1.call-done = bf16[16,105,1024]{2,1,0:T(8,128)(2,1)} async-done(((bf16[1,105,1024]{2,1,0:T(8,128)(2,1)}), bf16[16,105,1024]{2,1,0:T(8,128)(2,1)}) %all-gather.12.cloned.1.call-update) | async-done | bytes 3440656 | tf_op jit(solution)/shard_map/all_gather | solution.py:422
  105.9 1.5 collective-permute-start
  108.0 1.3 broadcast_in_dim.20.gain
  109.3 1.3 broadcast_in_dim.21.shift
  111.3 1.7 copy.42
  114.2 1.7 fusion.7
  117.2 1.5 fusion.6.upstream
  119.8 31.2 %collective-permute-done = bf16[750,1280]{1,0:T(8,128)(2,1)S(1)} collective-permute-done((bf16[750,1280]{1,0:T(8,128)(2,1)}, bf16[750,1280]{1,0:T(8,128)(2,1)S(1)}, u32[]{:S(2)}, u32[]{:S(2)}) %collective-permute-start) | collective-permute-done | bytes 1920032 | tf_op jit(solution)/shard_map/ppermute | solution.py:378
  151.5 2.4 pad_maximum_fusion.frames
  153.8 13.1 %encode.1 = (bf16[3,1536,320]{2,1,0:T(8,128)(2,1)}, f32[768,1280]{1,0:T(8,128)}) custom-call(bf16[1500,1280]{1,0:T(8,128)(2,1)} %pad_maximum_fusion.frames, f32[1,1280]{1,0:T(1,128)} %broadcast_in_dim.20.gain, f32[1,1280]{1,0:T(1,128)} %broadcast_in_dim.21.shift, bf16[16,3,80,320]{3,2,1,0:T(8,128)(2,1)} %bitcast.45), custom_call_target="tpu_custom_call" | custom-call | flops 3774873600 | bytes 14680064 | tf_op jit(solution)/shard_map/encode/pallas_call | solution.py:74
  168.1 1.5 collective-permute-start.3
  169.7 34.6 %encoder_attention.1 = bf16[768,320]{1,0:T(8,128)(2,1)} custom-call(s32[1]{0:T(128)S(6)} %copy.51.count, bf16[3,1536,320]{2,1,0:T(8,128)(2,1)} %get-tuple-element.14.queries.keys.values, bf16[3,1536,320]{2,1,0:T(8,128)(2,1)} %get-tuple-element.14.queries.keys.values, bf16[3,1536,320]{2,1,0:T(8,128)(2,1)} %get-tuple-element.14.queries.keys.values), custom_call_target="tpu_custom_call" | custom-call | flops 12079595520 | bytes 4194304 | tf_op jit(solution)/shard_map/encoder_attention/pallas_call | solution.py:117
  204.2 2.1 copy.35
  206.9 2.3 slice.20
  209.2 4.1 %reshape_reshape.3 = bf16[16,320,80]{2,1,0:T(8,128)(2,1)} reshape(bf16[16,25,1024]{2,1,0:T(8,128)(2,1)} %slice.20) | data formatting | bytes 1638400 | tf_op jit(solution)/shard_map/reshape;reshape | solution.py:429
  213.3 2.5 copy.38
  215.8 1.5 copy.40
  217.3 1.5 collective-permute-start.2
  219.8 2.1 fusion.3.text
  221.9 16.8 %collective-permute-done.1 = bf16[768,320]{0,1:T(8,128)(2,1)} collective-permute-done((bf16[768,320]{0,1:T(8,128)(2,1)}, bf16[768,320]{0,1:T(8,128)(2,1)}, u32[]{:S(2)}, u32[]{:S(2)}) %collective-permute-start.1) | collective-permute-done | bytes 491552 | tf_op jit(solution)/shard_map/ppermute | solution.py:378
  238.7 2.1 copy.36
  240.7 2.4 broadcast_select_fusion.6
  243.1 10.8 %collective-permute-done.2 = bf16[320,1280]{1,0:T(8,128)(2,1)} collective-permute-done((bf16[320,1280]{1,0:T(8,128)(2,1)S(1)}, bf16[320,1280]{1,0:T(8,128)(2,1)}, u32[]{:S(2)}, u32[]{:S(2)}) %collective-permute-start.2) | collective-permute-done | bytes 819232 | tf_op jit(solution)/shard_map/ppermute | solution.py:378
  253.9 1.3 broadcast_select_fusion.5
  255.2 1.3 pad_maximum_fusion.1.out_w
  256.5 4.4 %broadcast_select_fusion = (bf16[1280,1024]{1,0:T(8,128)(2,1)}, bf16[1280,1024]{1,0:T(8,128)(2,1)}) fusion(bf16[1280,1024]{1,0:T(8,128)(2,1)} %collective-permute-done.3, pred[]{:T(512)S(6)} %eq.2, bf16[16,80,1024]{2,1,0:T(8,128)(2,1)S(1)} %slice.21), kind=kLoop, calls=%fused_computation.10 | loop fusion | flops 2621440 | bytes 10485761 | tf_op jit(solution)/shard_map/jit(_where)/select_n | solution.py:380
  260.9 18.7 %embed.1 = (bf16[896,2048]{1,0:T(8,128)(2,1)}, bf16[896,128]{1,0:T(8,128)(2,1)}) custom-call(f32[768,1280]{1,0:T(8,128)} %get-tuple-element.13.pooled, bf16[768,320]{1,0:T(8,128)(2,1)} %get-tuple-element.33.context_a, bf16[768,320]{1,0:T(8,128)(2,1)} %get-tuple-element.32.context_b, bf16[640,1280]{1,0:T(8,128)(2,1)} %pad_maximum_fusion.1.out_w, ...), custom_call_target="tpu_custom_call" | custom-call | flops 9395240960 | bytes 25165824 | tf_op jit(solution)/shard_map/embed/pallas_call | solution.py:167
  279.6 47.3 %decoder.1 = (f32[2,64,1024]{2,1,0:T(8,128)}, f32[128,2048]{1,0:T(8,128)}) custom-call(s32[1]{0:T(128)S(6)} %copy.51.count, bf16[896,2048]{1,0:T(8,128)(2,1)} %get-tuple-element.17.normed, bf16[896,128]{1,0:T(8,128)(2,1)} %get-tuple-element.18.low, bf16[16,384,1024]{2,1,0:T(8,128)(2,1)} %bitcast.44, f32[2,64,1024]{2,1,0:T(8,128)} %up_w.1, ...), custom_call_target="tpu_custom_call" | custom-call | flops 18790481920 | bytes 25165824 | tf_op jit(solution)/shard_map/decoder/pallas_call | solution.py:276
  326.8 1.3 convert_element_type.51
  330.1 22.3 %reduce_terms.1 = f32[192,128]{1,0:T(8,128)} custom-call(bf16[16,192,128]{2,1,0:T(8,128)(2,1)} %pad_maximum_fusion.2.terms), custom_call_target="tpu_custom_call" | custom-call | tf_op jit(solution)/shard_map/reduce_terms/pallas_call | solution.py:349
  (52 shorter events, 14.3 us)
Async XLA Ops:
  7.2 105.8 %copy-start.6 = (f32[1280]{0:T(1024)S(1)}, f32[1280]{0:T(1024)}, u32[]{:S(2)}) copy-start(f32[1280]{0:T(1024)} %param.23) | copy-start | bytes 15364
  7.2 106.4 %copy-start.7 = (f32[1280]{0:T(1024)S(1)}, f32[1280]{0:T(1024)}, u32[]{:S(2)}) copy-start(f32[1280]{0:T(1024)} %param.24) | copy-start | bytes 15364
  7.2 50.6 %all-gather.8.cloned.1.call-start = ((), (), s32[]{:S(2)}) async-start(), calls=%async_computation | async-start | bytes 3133440 | tf_op jit(solution)/shard_map/all_gather | solution.py:403
  7.9 98.0 %all-gather.12.cloned.1.call-start = ((), (), s32[]{:S(2)}) async-start(), calls=%async_computation.2 | async-start | bytes 3899392 | tf_op jit(solution)/shard_map/all_gather | solution.py:422
  57.8 221.8 %all-gather.10.cloned.1.call-start = ((), (), s32[]{:S(2)}) async-start(), calls=%async_computation.1 | async-start | bytes 13369344 | tf_op jit(solution)/shard_map/all_gather | solution.py:427
  105.9 45.0 %collective-permute-start = (bf16[750,1280]{1,0:T(8,128)(2,1)}, bf16[750,1280]{1,0:T(8,128)(2,1)S(1)}, u32[]{:S(2)}, u32[]{:S(2)}) collective-permute-start(bf16[750,1280]{1,0:T(8,128)(2,1)} %bitcast.35), channel_id=1, source_target_pairs={{0,1},{1,0},{2,3},{3,2},{4,5},{5,4},{6,7},{7,6},{8,9},{9,8},{10,11... | collective-permute-start | bytes 5760008 | tf_op jit(solution)/shard_map/ppermute | solution.py:378
  107.5 111.4 %collective-permute-start.4 = (bf16[21,2048]{1,0:T(8,128)(2,1)}, bf16[21,2048]{1,0:T(8,128)(2,1)}, u32[]{:S(2)}, u32[]{:S(2)}) collective-permute-start(bf16[21,2048]{1,0:T(8,128)(2,1)} %bitcast.42), channel_id=1, source_target_pairs={{0,1},{1,0},{2,3},{3,2},{4,5},{5,4},{6,7},{7,6},{8,9},{9,8},{10,11... | collective-permute-start | bytes 258056 | tf_op jit(solution)/shard_map/ppermute | solution.py:378
  111.2 5.9 %copy-start.5 = (bf16[1,42,1024]{2,1,0:T(8,128)(2,1)S(1)}, bf16[1,42,1024]{2,1,0:T(8,128)(2,1)}, u32[]{:S(2)}) copy-start(bf16[1,42,1024]{2,1,0:T(8,128)(2,1)} %param.33) | copy-start | bytes 258052
  114.2 3.0 copy-start.2
  118.6 32.4 %copy-start.1 = (bf16[1,750,1280]{2,1,0:T(8,128)(2,1)S(1)}, bf16[1,750,1280]{2,1,0:T(8,128)(2,1)}, u32[]{:S(2)}) copy-start(bf16[1,750,1280]{2,1,0:T(8,128)(2,1)} %param.17) | copy-start | bytes 5760004
  153.8 13.1 %copy-start = (bf16[16,105,1024]{2,1,0:T(8,128)(2,1)S(1)}, bf16[16,105,1024]{2,1,0:T(8,128)(2,1)}, u32[]{:S(2)}) copy-start(bf16[16,105,1024]{2,1,0:T(8,128)(2,1)} %all-gather.12.cloned.1.call-done) | copy-start | bytes 10321924
  168.1 88.4 %collective-permute-start.3 = (bf16[1280,1024]{1,0:T(8,128)(2,1)S(1)}, bf16[1280,1024]{1,0:T(8,128)(2,1)}, u32[]{:S(2)}, u32[]{:S(2)}) collective-permute-start(bf16[1280,1024]{1,0:T(8,128)(2,1)S(1)} %bitcast.30), channel_id=1, source_target_pairs={{0,1},{1,0},{2,3},{3,2},{4,5},{5,4},{6,7},{7,6},{8,9},{9,8},{10,11... | collective-permute-start | bytes 7864328 | tf_op jit(solution)/shard_map/ppermute | solution.py:378
  206.3 32.3 %collective-permute-start.1 = (bf16[768,320]{0,1:T(8,128)(2,1)}, bf16[768,320]{0,1:T(8,128)(2,1)}, u32[]{:S(2)}, u32[]{:S(2)}) collective-permute-start(bf16[768,320]{0,1:T(8,128)(2,1)} %copy.35), channel_id=1, source_target_pairs={{0,1},{1,0},{2,3},{3,2},{4,5},{5,4},{6,7},{7,6},{8,9},{9,8},{10,11... | collective-permute-start | bytes 1474568 | tf_op jit(solution)/shard_map/ppermute | solution.py:378
  213.3 5.5 %copy-start.4 = (bf16[1,21,2048]{2,1,0:T(8,128)(2,1)S(1)}, bf16[1,21,2048]{2,1,0:T(8,128)(2,1)}, u32[]{:S(2)}) copy-start(bf16[1,21,2048]{2,1,0:T(8,128)(2,1)} %param.27) | copy-start | bytes 258052
  217.3 36.6 %collective-permute-start.2 = (bf16[320,1280]{1,0:T(8,128)(2,1)S(1)}, bf16[320,1280]{1,0:T(8,128)(2,1)}, u32[]{:S(2)}, u32[]{:S(2)}) collective-permute-start(bf16[320,1280]{1,0:T(8,128)(2,1)S(1)} %copy.40), channel_id=1, source_target_pairs={{0,1},{1,0},{2,3},{3,2},{4,5},{5,4},{6,7},{7,6},{8,9},{9,8},{10,11... | collective-permute-start | bytes 2457608 | tf_op jit(solution)/shard_map/ppermute | solution.py:378
  326.8 1.9 copy-start.3
Sparse Core Ops, SparseCore 0:
  10.2 47.5 all-gather.7
  60.0 45.8 all-gather.11
  108.2 99.7 all-gather.9

commit v2 on v1

--- a/solution.py
+++ b/solution.py
@@ -416,22 +416,21 @@
     flat = encoder_out.reshape(-1)
     flat = jnp.pad(flat, (0, round_up(flat.size, columns) - flat.size))
     late = jnp.concatenate([flat.reshape(-1, columns), projector], 0)
-    encoder_w, late = lax.optimization_barrier((encoder_w, late))
+    all_frames, late = lax.optimization_barrier((all_frames, late))
     if encoder_w.shape[2] % 16:
         encoder_w = encoder_w.transpose(1, 0, 2, 3).reshape(1, 3, -1, encoder_w.shape[3])
     late = lax.all_gather(late, "dp")
     split = late.shape[1] - projector.shape[0]
-    late, decoder_rows = lax.optimization_barrier(
-        (late, decoder_qkv.reshape(3 * deep, columns))
+    triple, pooled = encode(all_frames, encoder_gain, encoder_shift, encoder_w)
+    triple, decoder_rows = lax.optimization_barrier(
+        (triple, decoder_qkv.reshape(3 * deep, columns))
     )
     decoder_w = lax.all_gather(decoder_rows, "dp")
+    context = encoder_attention(triple, frame_counts)
     out_half = late[:, :split].reshape(parts, -1)[:, :encoder_out.size]
     out_half = out_half.reshape((parts,) + encoder_out.shape).transpose(1, 0, 2)
     out_w = jnp.concatenate(both(out_half.reshape(encoder_out.shape[0], -1), 0), 0)
     proj_a, proj_b = both(late[:, split:].reshape(-1, columns), 1)
-
-    triple, pooled = encode(all_frames, encoder_gain, encoder_shift, encoder_w)
-    context = encoder_attention(triple, frame_counts)
     context_a, context_b = both(context, 1)
     low_w = jnp.concatenate([adapter_in[0], adapter_in[1]], 1).astype(BF16)
     normed, low = embed(

time: 365 us -> 308 us (0.84)
  waiting for transfers between devices: 155 us -> 92.9 us
    all_gather x1, waiting for transfers between devices: 47 us -> 0.01 us  [per_device(): encoder_w = lax.all_gather(encoder_qkv, 'dp')]
    all_gather x1, waiting for transfers between devices: 48.1 us -> 23.7 us  [per_device(): late = lax.all_gather(late, 'dp')]
    ppermute x5, waiting for transfers between devices: 58.8 us -> 68.5 us  [both(): other = lax.ppermute(value, 'tensor', [(0, 1), (1, 0)])]
  transfers between devices with their start and end apart: 8 -> 8, of which waited for: 5 -> 4; matrix products, arithmetic and copies ran while one was open for 12% -> 15% of each run, Pallas kernels for 18% -> 22%
where the time goes in v2:
time: 308 us; the launch traced here: 305 us
  Pallas kernels  135 us (44%)
  waiting for transfers between devices  92.9 us (30%)
  local copies, waits for them, and re-layouts  26.9 us (9%)
  other arithmetic  26.3 us (9%)
  between operations  14.6 us (5%)
  starting transfers between devices  8.58 us (3%)
    ppermute x5, waiting for transfers between devices, both(): other = lax.ppermute(value, 'tensor', [(0, 1), (1, 0)])  68.5 us
    pallas_call x1, Pallas kernels, decoder(): pl.pallas_call(functools.partial(decoder_kernel, audio), grid=(all_column...  47.3 us
    pallas_call x1, Pallas kernels, encoder_attention(): pl.pallas_call(encoder_attention_kernel, grid=(padded // tile,), in_specs...  34.5 us
    all_gather x1, waiting for transfers between devices, per_device(): late = lax.all_gather(late, 'dp')  23.7 us
    pallas_call x1, Pallas kernels, reduce_terms(): pl.pallas_call(functools.partial(reduce_kernel, parts, shared), out_shape...  22 us
    pallas_call x1, Pallas kernels, embed(): pl.pallas_call(functools.partial(embed_kernel, audio), grid=(total // til...  18.7 us
    pallas_call x1, Pallas kernels, encode(): pl.pallas_call(functools.partial(encode_kernel, length), grid=(padded //...  13 us
    select_n x5, other arithmetic, both(): return (jnp.where(first, value, other), jnp.where(first, other, value))  11 us
  transfers between devices with their start and end apart: 8, of which 4 were waited for; matrix products, arithmetic and copies ran while one was open for 15% of the time, Pallas kernels for 22%

profile of v2, /device:TPU:0, one launch (start us, length us, event | category | flops | bytes accessed | tf_op | source)
XLA Modules:
  0.0 304.8 jit_solution(8294909622436490513)
XLA Ops:
  7.9 3.0 collective-permute-start
  12.1 1.7 pad_maximum_fusion.6
  13.8 39.4 %collective-permute-done = bf16[750,1280]{1,0:T(8,128)(2,1)S(1)} collective-permute-done((bf16[750,1280]{1,0:T(8,128)(2,1)}, bf16[750,1280]{1,0:T(8,128)(2,1)S(1)}, u32[]{:S(2)}, u32[]{:S(2)}) %collective-permute-start) | collective-permute-done | bytes 1920032 | tf_op jit(solution)/shard_map/ppermute | solution.py:378
  53.1 1.8 broadcast_select_fusion.3
  54.9 2.4 pad_maximum_fusion.frames
  58.6 13.0 %encode.1 = (bf16[3,1536,320]{2,1,0:T(8,128)(2,1)}, f32[768,1280]{1,0:T(8,128)}) custom-call(bf16[1500,1280]{1,0:T(8,128)(2,1)} %pad_maximum_fusion.frames, f32[1,1280]{1,0:T(1,128)} %broadcast_in_dim.20.gain, f32[1,1280]{1,0:T(1,128)} %broadcast_in_dim.21.shift, bf16[16,3,80,320]{3,2,1,0:T(8,128)(2,1)} %bitcast.45), custom_call_target="tpu_custom_call" | custom-call | flops 3774873600 | bytes 14680064 | tf_op jit(solution)/shard_map/encode/pallas_call | solution.py:74
  71.7 1.8 collective-permute-start.4
  74.2 1.8 copy.42
  77.2 1.7 fusion.7
  80.2 1.5 fusion.6.upstream
  82.8 23.7 %all-gather.12.cloned.1.call-done = bf16[16,105,1024]{2,1,0:T(8,128)(2,1)} async-done(((bf16[1,105,1024]{2,1,0:T(8,128)(2,1)}), bf16[16,105,1024]{2,1,0:T(8,128)(2,1)}) %all-gather.12.cloned.1.call-update) | async-done | bytes 3440656 | tf_op jit(solution)/shard_map/all_gather | solution.py:422
  106.5 3.0 slice.27
  109.5 1.5 collective-permute-start.3
  111.0 34.5 %encoder_attention.1 = bf16[768,320]{1,0:T(8,128)(2,1)} custom-call(s32[1]{0:T(128)S(6)} %copy.51.count, bf16[3,1536,320]{2,1,0:T(8,128)(2,1)} %get-tuple-element.15.queries.keys.values, bf16[3,1536,320]{2,1,0:T(8,128)(2,1)} %get-tuple-element.15.queries.keys.values, bf16[3,1536,320]{2,1,0:T(8,128)(2,1)} %get-tuple-element.15.queries.keys.values), custom_call_target="tpu_custom_call" | custom-call | flops 12079595520 | bytes 4194304 | tf_op jit(solution)/shard_map/encoder_attention/pallas_call | solution.py:117
  145.6 2.1 copy.35
  148.2 2.3 slice.26
  150.5 4.2 %reshape_reshape.3 = bf16[16,320,80]{2,1,0:T(8,128)(2,1)} reshape(bf16[16,25,1024]{2,1,0:T(8,128)(2,1)} %slice.26) | data formatting | bytes 1638400 | tf_op jit(solution)/shard_map/reshape;reshape | solution.py:431
  154.7 2.4 copy.38
  157.1 1.5 copy.40
  158.6 1.5 collective-permute-start.2
  161.1 2.1 fusion.3.text
  163.2 16.7 %collective-permute-done.1 = bf16[768,320]{0,1:T(8,128)(2,1)} collective-permute-done((bf16[768,320]{0,1:T(8,128)(2,1)}, bf16[768,320]{0,1:T(8,128)(2,1)}, u32[]{:S(2)}, u32[]{:S(2)}) %collective-permute-start.1) | collective-permute-done | bytes 491552 | tf_op jit(solution)/shard_map/ppermute | solution.py:378
  179.9 2.1 copy.36
  182.0 2.4 broadcast_select_fusion.6
  184.4 12.4 %collective-permute-done.2 = bf16[320,1280]{1,0:T(8,128)(2,1)} collective-permute-done((bf16[320,1280]{1,0:T(8,128)(2,1)S(1)}, bf16[320,1280]{1,0:T(8,128)(2,1)}, u32[]{:S(2)}, u32[]{:S(2)}) %collective-permute-start.2) | collective-permute-done | bytes 819232 | tf_op jit(solution)/shard_map/ppermute | solution.py:378
  196.8 1.3 broadcast_select_fusion.5
  198.0 1.3 pad_maximum_fusion.1.out_w
  199.3 4.6 %broadcast_select_fusion = (bf16[1280,1024]{1,0:T(8,128)(2,1)}, bf16[1280,1024]{1,0:T(8,128)(2,1)}) fusion(bf16[1280,1024]{1,0:T(8,128)(2,1)} %collective-permute-done.3, pred[]{:T(512)S(6)} %eq.2, bf16[16,80,1024]{2,1,0:T(8,128)(2,1)S(1)} %slice.27), kind=kLoop, calls=%fused_computation.10 | loop fusion | flops 2621440 | bytes 10485761 | tf_op jit(solution)/shard_map/jit(_where)/select_n | solution.py:380
  204.0 18.7 %embed.1 = (bf16[896,2048]{1,0:T(8,128)(2,1)}, bf16[896,128]{1,0:T(8,128)(2,1)}) custom-call(f32[768,1280]{1,0:T(8,128)} %get-tuple-element.13.pooled, bf16[768,320]{1,0:T(8,128)(2,1)} %get-tuple-element.33.context_a, bf16[768,320]{1,0:T(8,128)(2,1)} %get-tuple-element.32.context_b, bf16[640,1280]{1,0:T(8,128)(2,1)} %pad_maximum_fusion.1.out_w, ...), custom_call_target="tpu_custom_call" | custom-call | flops 9395240960 | bytes 25165824 | tf_op jit(solution)/shard_map/embed/pallas_call | solution.py:167
  222.7 47.3 %decoder.1 = (f32[2,64,1024]{2,1,0:T(8,128)}, f32[128,2048]{1,0:T(8,128)}) custom-call(s32[1]{0:T(128)S(6)} %copy.51.count, bf16[896,2048]{1,0:T(8,128)(2,1)} %get-tuple-element.17.normed, bf16[896,128]{1,0:T(8,128)(2,1)} %get-tuple-element.18.low, bf16[16,384,1024]{2,1,0:T(8,128)(2,1)} %bitcast.44, f32[2,64,1024]{2,1,0:T(8,128)} %up_w.1, ...), custom_call_target="tpu_custom_call" | custom-call | flops 18790481920 | bytes 25165824 | tf_op jit(solution)/shard_map/decoder/pallas_call | solution.py:276
  270.0 1.3 convert_element_type.51
  273.2 22.0 %reduce_terms.1 = f32[192,128]{1,0:T(8,128)} custom-call(bf16[16,192,128]{2,1,0:T(8,128)(2,1)} %pad_maximum_fusion.2.terms), custom_call_target="tpu_custom_call" | custom-call | tf_op jit(solution)/shard_map/reduce_terms/pallas_call | solution.py:349
  (52 shorter events, 13.2 us)
Async XLA Ops:
  7.2 51.5 %all-gather.8.cloned.1.call-start = ((), (), s32[]{:S(2)}) async-start(), calls=%async_computation | async-start | bytes 3133440 | tf_op jit(solution)/shard_map/all_gather | solution.py:403
  7.9 98.6 %all-gather.12.cloned.1.call-start = ((), (), s32[]{:S(2)}) async-start(), calls=%async_computation.2 | async-start | bytes 3899392 | tf_op jit(solution)/shard_map/all_gather | solution.py:422
  7.9 45.2 %collective-permute-start = (bf16[750,1280]{1,0:T(8,128)(2,1)}, bf16[750,1280]{1,0:T(8,128)(2,1)S(1)}, u32[]{:S(2)}, u32[]{:S(2)}) collective-permute-start(bf16[750,1280]{1,0:T(8,128)(2,1)} %bitcast.35), channel_id=1, source_target_pairs={{0,1},{1,0},{2,3},{3,2},{4,5},{5,4},{6,7},{7,6},{8,9},{9,8},{10,11... | collective-permute-start | bytes 5760008 | tf_op jit(solution)/shard_map/ppermute | solution.py:378
  54.9 2.5 copy-start.4
  54.9 3.1 %copy-start.5 = (f32[1280]{0:T(1024)S(1)}, f32[1280]{0:T(1024)}, u32[]{:S(2)}) copy-start(f32[1280]{0:T(1024)} %param.20) | copy-start | bytes 15364
  57.4 165.3 %all-gather.10.cloned.1.call-start = ((), (), s32[]{:S(2)}) async-start(), calls=%async_computation.1 | async-start | bytes 13369344 | tf_op jit(solution)/shard_map/all_gather | solution.py:428
  58.6 13.1 %copy-start.2 = (bf16[1,21,2048]{2,1,0:T(8,128)(2,1)S(1)}, bf16[1,21,2048]{2,1,0:T(8,128)(2,1)}, u32[]{:S(2)}) copy-start(bf16[1,21,2048]{2,1,0:T(8,128)(2,1)} %param.27) | copy-start | bytes 258052
  71.7 4.3 %copy-start.6 = (f32[1280]{0:T(1024)S(1)}, f32[1280]{0:T(1024)}, u32[]{:S(2)}) copy-start(f32[1280]{0:T(1024)} %param.23) | copy-start | bytes 15364
  71.7 5.0 %copy-start.7 = (f32[1280]{0:T(1024)S(1)}, f32[1280]{0:T(1024)}, u32[]{:S(2)}) copy-start(f32[1280]{0:T(1024)} %param.24) | copy-start | bytes 15364
  71.7 88.5 %collective-permute-start.4 = (bf16[21,2048]{1,0:T(8,128)(2,1)S(1)}, bf16[21,2048]{1,0:T(8,128)(2,1)}, u32[]{:S(2)}, u32[]{:S(2)}) collective-permute-start(bf16[21,2048]{1,0:T(8,128)(2,1)S(1)} %bitcast.42), channel_id=1, source_target_pairs={{0,1},{1,0},{2,3},{3,2},{4,5},{5,4},{6,7},{7,6},{8,9},{9,8},{10,11... | collective-permute-start | bytes 258056 | tf_op jit(solution)/shard_map/ppermute | solution.py:378
  74.2 6.0 %copy-start = (bf16[1,750,1024]{2,1,0:T(8,128)(2,1)S(1)}, bf16[1,750,1024]{2,1,0:T(8,128)(2,1)}, u32[]{:S(2)}) copy-start(bf16[1,750,1024]{2,1,0:T(8,128)(2,1)} %param.32) | copy-start | bytes 4608004
  74.2 6.0 %copy-start.3 = (bf16[1,42,1024]{2,1,0:T(8,128)(2,1)S(1)}, bf16[1,42,1024]{2,1,0:T(8,128)(2,1)}, u32[]{:S(2)}) copy-start(bf16[1,42,1024]{2,1,0:T(8,128)(2,1)} %param.33) | copy-start | bytes 258052
  109.5 89.8 %collective-permute-start.3 = (bf16[1280,1024]{1,0:T(8,128)(2,1)S(1)}, bf16[1280,1024]{1,0:T(8,128)(2,1)}, u32[]{:S(2)}, u32[]{:S(2)}) collective-permute-start(bf16[1280,1024]{1,0:T(8,128)(2,1)S(1)} %bitcast.30), channel_id=1, source_target_pairs={{0,1},{1,0},{2,3},{3,2},{4,5},{5,4},{6,7},{7,6},{8,9},{9,8},{10,11... | collective-permute-start | bytes 7864328 | tf_op jit(solution)/shard_map/ppermute | solution.py:378
  147.6 32.3 %collective-permute-start.1 = (bf16[768,320]{0,1:T(8,128)(2,1)}, bf16[768,320]{0,1:T(8,128)(2,1)}, u32[]{:S(2)}, u32[]{:S(2)}) collective-permute-start(bf16[768,320]{0,1:T(8,128)(2,1)} %copy.35), channel_id=1, source_target_pairs={{0,1},{1,0},{2,3},{3,2},{4,5},{5,4},{6,7},{7,6},{8,9},{9,8},{10,11... | collective-permute-start | bytes 1474568 | tf_op jit(solution)/shard_map/ppermute | solution.py:378
  158.6 38.1 %collective-permute-start.2 = (bf16[320,1280]{1,0:T(8,128)(2,1)S(1)}, bf16[320,1280]{1,0:T(8,128)(2,1)}, u32[]{:S(2)}, u32[]{:S(2)}) collective-permute-start(bf16[320,1280]{1,0:T(8,128)(2,1)S(1)} %copy.40), channel_id=1, source_target_pairs={{0,1},{1,0},{2,3},{3,2},{4,5},{5,4},{6,7},{7,6},{8,9},{9,8},{10,11... | collective-permute-start | bytes 2457608 | tf_op jit(solution)/shard_map/ppermute | solution.py:378
  270.0 1.9 copy-start.1
Sparse Core Ops, SparseCore 0:
  10.2 47.5 all-gather.7
  60.0 46.4 all-gather.11
  108.8 99.8 all-gather.9

commit v3 on v2

--- a/solution.py
+++ b/solution.py
@@ -68,8 +68,8 @@
 def encode(frames, gain, shift, weights):
     length, width = frames.shape
     parts, _, depth, columns = weights.shape
-    tile = 256
-    padded = round_up(length, 2 * tile)
+    tile = 512
+    padded = round_up(length, tile)
     whole = lambda shape: pl.BlockSpec(shape, lambda i: (0,) * len(shape))
     return pl.pallas_call(
         functools.partial(encode_kernel, length),
@@ -159,8 +159,8 @@
           text, root_gain, low_w):
     total, features = text.shape
     width = pooled.shape[1]
-    tile = 128
-    last = pooled.shape[0] // tile - 1
+    tile = total // 2
+    last = -(-pooled.shape[0] // tile) - 1
     whole = lambda shape: pl.BlockSpec(shape, lambda i: (0,) * len(shape))
     held = lambda i: (jnp.minimum(i, last), 0)
     row = lambda i: (i, 0)
@@ -366,6 +366,93 @@
     )(terms)
 
 
+def ring_index(place, parts):
+    half = parts // 2
+    row = lax.div(place, half)
+    step = place - row * half
+    core = lax.rem(step, 2)
+    level = lax.div(step, 2)
+    level = (1 - row) * level + row * (parts // 4 - 1 - level)
+    return level * 4 + row * 2 + core
+
+
+def ring_place(index, parts):
+    core = lax.rem(index, 2)
+    row = lax.rem(lax.div(index, 2), 2)
+    level = lax.div(index, 4)
+    level = (1 - row) * level + row * (parts // 4 - 1 - level)
+    return row * (parts // 2) + level * 2 + core
+
+
+def ring_kernel(parts, count, *refs):
+    shards, wholes = refs[:count], refs[count:2 * count]
+    local_sem, send_sem, recv_sem = refs[2 * count:]
+    me = lax.axis_index("dp")
+    tensor = lax.axis_index("tensor")
+    place = ring_place(me, parts)
+    right = ring_index(lax.rem(place + 1, parts), parts)
+    left = ring_index(lax.rem(place + parts - 1, parts), parts)
+    barrier = pltpu.get_barrier_semaphore()
+    for peer in (left, right):
+        pl.semaphore_signal(barrier, inc=1, device_id=(peer, tensor), device_id_type=MESH)
+    pl.semaphore_wait(barrier, 2)
+    own = []
+    for i in range(count):
+        copy = pltpu.make_async_copy(shards[i], wholes[i].at[me], local_sem.at[i])
+        copy.start()
+        own.append(copy)
+    sent = []
+    before = {}
+    ways = ((right, parts // 2, parts - 1), (left, parts - 1 - parts // 2, 1))
+    for step in range(parts // 2):
+        for i in range(count):
+            for way, (peer, steps, turn) in enumerate(ways):
+                if step >= steps:
+                    continue
+                if step > 0:
+                    before[way, i].wait_recv()
+                owner = ring_index(lax.rem(place + step * turn, parts), parts)
+                copy = pltpu.make_async_remote_copy(
+                    src_ref=shards[i] if step == 0 else wholes[i].at[owner],
+                    dst_ref=wholes[i].at[owner],
+                    send_sem=send_sem.at[way, step, i],
+                    recv_sem=recv_sem.at[way, step, i],
+                    device_id=(peer, tensor),
+                    device_id_type=MESH,
+                )
+                copy.start()
+                sent.append(copy)
+                before[way, i] = copy
+    for copy in before.values():
+        copy.wait_recv()
+    for copy in sent:
+        copy.wait_send()
+    for copy in own:
+        copy.wait()
+
+
+def ring_gather(shards):
+    parts = lax.axis_size("dp")
+    count = len(shards)
+    anywhere = pl.BlockSpec(memory_space=pl.ANY)
+    return pl.pallas_call(
+        functools.partial(ring_kernel, parts, count),
+        out_shape=[jax.ShapeDtypeStruct((parts,) + s.shape, s.dtype) for s in shards],
+        in_specs=[anywhere] * count,
+        out_specs=[anywhere] * count,
+        scratch_shapes=[
+            pltpu.SemaphoreType.DMA((count,)),
+            pltpu.SemaphoreType.DMA((2, parts // 2, count)),
+            pltpu.SemaphoreType.DMA((2, parts // 2, count)),
+        ],
+        compiler_params=pltpu.CompilerParams(
+            collective_id=1, has_side_effects=True, vmem_limit_bytes=VMEM_BYTES
+        ),
+        cost_estimate=pl.CostEstimate(flops=0, bytes_accessed=128 * 2**20, transcendentals=0),
+        name="ring_gather",
+    )(*shards)
+
+
 def rope_tables(length):
     position = jnp.arange(length).astype(F32)
     frequency = ROPE_BASE ** (-jnp.arange(0, HD, 2).astype(F32) / HD)
@@ -400,37 +487,30 @@
     text_upstream,
 ):
     parts = lax.axis_size("dp")
-    encoder_w = lax.all_gather(encoder_qkv, "dp")
     audio, columns = audio_upstream.shape[1:]
     text_rows = text_upstream.shape[1]
     total = round_up(audio + text_rows, 128)
     tail = total - audio - text_rows
-
+    deep = decoder_qkv.shape[1]
+
+    decoder_w = lax.all_gather(decoder_qkv.reshape(3 * deep, columns), "dp")
     all_frames = jnp.concatenate(both(frames[0], 0), 0)
+    shards = [encoder_qkv, encoder_out, projector]
+    if parts % 4 == 0 and encoder_qkv.shape[1] % 16 == 0:
+        encoder_w, out_parts, proj_parts = ring_gather(shards)
+    else:
+        encoder_w, out_parts, proj_parts = [lax.all_gather(s, "dp") for s in shards]
+        encoder_w = encoder_w.transpose(1, 0, 2, 3).reshape(1, 3, -1, encoder_w.shape[3])
+    out_half = out_parts.transpose(1, 0, 2).reshape(encoder_out.shape[0], -1)
+    proj_a, proj_b = both(proj_parts.reshape(-1, columns), 1)
+    out_w = jnp.concatenate(both(out_half, 0), 0)
     text = jnp.concatenate(both(text_embed[0], 0), 0)
     text = jnp.pad(text, ((audio, tail), (0, 0)))
     upstream = jnp.pad(
         jnp.concatenate([audio_upstream[0], text_upstream[0]], 0), ((0, tail), (0, 0))
     )
-    deep = decoder_qkv.shape[1]
-    flat = encoder_out.reshape(-1)
-    flat = jnp.pad(flat, (0, round_up(flat.size, columns) - flat.size))
-    late = jnp.concatenate([flat.reshape(-1, columns), projector], 0)
-    all_frames, late = lax.optimization_barrier((all_frames, late))
-    if encoder_w.shape[2] % 16:
-        encoder_w = encoder_w.transpose(1, 0, 2, 3).reshape(1, 3, -1, encoder_w.shape[3])
-    late = lax.all_gather(late, "dp")
-    split = late.shape[1] - projector.shape[0]
     triple, pooled = encode(all_frames, encoder_gain, encoder_shift, encoder_w)
-    triple, decoder_rows = lax.optimization_barrier(
-        (triple, decoder_qkv.reshape(3 * deep, columns))
-    )
-    decoder_w = lax.all_gather(decoder_rows, "dp")
     context = encoder_attention(triple, frame_counts)
-    out_half = late[:, :split].reshape(parts, -1)[:, :encoder_out.size]
-    out_half = out_half.reshape((parts,) + encoder_out.shape).transpose(1, 0, 2)
-    out_w = jnp.concatenate(both(out_half.reshape(encoder_out.shape[0], -1), 0), 0)
-    proj_a, proj_b = both(late[:, split:].reshape(-1, columns), 1)
     context_a, context_b = both(context, 1)
     low_w = jnp.concatenate([adapter_in[0], adapter_in[1]], 1).astype(BF16)
     normed, low = embed(

time: 308 us -> 375 us (1.22)
  Pallas kernels: 135 us -> 246 us
  waiting for transfers between devices: 92.9 us -> 64 us
  local copies, waits for them, and re-layouts: 26.9 us -> 16.3 us
    pallas_call x0 -> x1, Pallas kernels: none -> 75 us  [ring_gather(): pl.pallas_call(functools.partial(ring_kernel, parts, count), out_shape=[j...]
    pallas_call x1, Pallas kernels: 22 us -> 58.5 us  [reduce_terms(): pl.pallas_call(functools.partial(reduce_kernel, parts, shared), out_shape...]
    all_gather x3 -> x1, waiting for transfers between devices: 23.7 us -> 0.01 us  [per_device(): decoder_w = lax.all_gather(decoder_qkv.reshape(3 * deep, columns), 'dp')]
    slice x2 -> x0, local copies, waits for them, and re-layouts: 5.27 us -> none  [the longest x1 2.97 us: per_device(): proj_a, proj_b = both(late[:, split:].reshape(-1, columns), 1)]
    ppermute x5, waiting for transfers between devices: 68.5 us -> 63.4 us  [both(): other = lax.ppermute(value, 'tensor', [(0, 1), (1, 0)])]
    another operation x1 -> x0, local copies, waits for them, and re-layouts: 4.25 us -> none  [per_device(): out_half = out_half.reshape((parts,) + encoder_out.shape).transpose(1, 0, 2)]
  transfers between devices with their start and end apart: 8 -> 6, of which waited for: 4 -> 2; matrix products, arithmetic and copies ran while one was open for 15% -> 10% of each run, Pallas kernels for 22% -> 38%
where the time goes in v3:
time: 375 us; the launch traced here: 372 us
  Pallas kernels  246 us (66%)
  waiting for transfers between devices  64 us (17%)
  other arithmetic  25.4 us (7%)
  local copies, waits for them, and re-layouts  16.3 us (4%)
  between operations  14.9 us (4%)
  starting transfers between devices  5.24 us (1%)
    pallas_call x1, Pallas kernels, ring_gather(): pl.pallas_call(functools.partial(ring_kernel, parts, count), out_shape=[j...  75 us
    ppermute x5, waiting for transfers between devices, both(): other = lax.ppermute(value, 'tensor', [(0, 1), (1, 0)])  63.4 us
    pallas_call x1, Pallas kernels, reduce_terms(): pl.pallas_call(functools.partial(reduce_kernel, parts, shared), out_shape...  58.5 us
    pallas_call x1, Pallas kernels, decoder(): pl.pallas_call(functools.partial(decoder_kernel, audio), grid=(all_column...  47.4 us
    pallas_call x1, Pallas kernels, encoder_attention(): pl.pallas_call(encoder_attention_kernel, grid=(padded // tile,), in_specs...  34.5 us
    pallas_call x1, Pallas kernels, embed(): pl.pallas_call(functools.partial(embed_kernel, audio), grid=(total // til...  17.3 us
    pallas_call x1, Pallas kernels, encode(): pl.pallas_call(functools.partial(encode_kernel, length), grid=(padded //...  13 us
    select_n x5, other arithmetic, both(): return (jnp.where(first, value, other), jnp.where(first, other, value))  10.8 us
  transfers between devices with their start and end apart: 6, of which 2 were waited for; matrix products, arithmetic and copies ran while one was open for 10% of the time, Pallas kernels for 38%

profile of v3, /device:TPU:0, one launch (start us, length us, event | category | flops | bytes accessed | tf_op | source)
XLA Modules:
  0.0 371.6 jit_solution(9764254470259284879)
XLA Ops:
  7.2 0.7 all-gather.2.cloned.1.call-update
  7.9 3.0 collective-permute-start
  10.9 1.6 copy.34.refs_1_
  12.5 75.0 %ring_gather.1 = (bf16[16,3,80,320]{3,2,1,0:T(8,128)(2,1)}, bf16[16,320,80]{2,1,0:T(8,128)(2,1)}, bf16[16,80,1024]{2,1,0:T(8,128)(2,1)}) custom-call(bf16[3,80,320]{2,1,0:T(8,128)(2,1)} %refs_0_.1, bf16[320,80]{1,0:T(8,128)(2,1)} %copy.34.refs_1_, bf16[80,1024]{1,0:T(8,128)(2,1)} %refs_2_.1), custom_call_target="tpu_custom_call" | custom-call | bytes 134217728 | tf_op jit(solution)/shard_map/ring_gather/pallas_call | solution.py:438
  87.5 1.8 copy.38
  90.1 2.0 collective-permute-start.3
  94.0 1.7 copy.42
  97.0 2.4 fusion.6.upstream
  99.4 1.1 pad_maximum_fusion.3.low_w
  100.5 1.7 fusion.7
  102.2 1.3 pad_maximum_fusion.4
  103.4 56.9 %collective-permute-done.4 = bf16[21,2048]{1,0:T(8,128)(2,1)} collective-permute-done((bf16[21,2048]{1,0:T(8,128)(2,1)S(1)}, bf16[21,2048]{1,0:T(8,128)(2,1)}, u32[]{:S(2)}, u32[]{:S(2)}) %collective-permute-start.4) | collective-permute-done | bytes 86048 | tf_op jit(solution)/shard_map/ppermute | solution.py:465
  160.3 0.9 broadcast_select_fusion.9
  161.2 2.1 fusion.3.text
  163.4 2.0 broadcast_select_fusion.3
  165.4 2.4 pad_maximum_fusion.frames
  167.8 13.0 %encode.1 = (bf16[3,1536,320]{2,1,0:T(8,128)(2,1)}, f32[768,1280]{1,0:T(8,128)}) custom-call(bf16[1500,1280]{1,0:T(8,128)(2,1)} %pad_maximum_fusion.frames, f32[1,1280]{1,0:T(1,128)} %broadcast_in_dim.20.gain, f32[1,1280]{1,0:T(1,128)} %broadcast_in_dim.21.shift, bf16[16,3,80,320]{3,2,1,0:T(8,128)(2,1)} %get-tuple-element.11.weights), custom_call_target="tpu_custom_call" | custom-call | flops 3774873600 | bytes 14680064 | tf_op jit(solution)/shard_map/encode/pallas_call | solution.py:74
  180.8 34.5 %encoder_attention.1 = bf16[768,320]{1,0:T(8,128)(2,1)} custom-call(s32[1]{0:T(128)S(6)} %copy.51.count, bf16[3,1536,320]{2,1,0:T(8,128)(2,1)} %get-tuple-element.13.queries.keys.values, bf16[3,1536,320]{2,1,0:T(8,128)(2,1)} %get-tuple-element.13.queries.keys.values, bf16[3,1536,320]{2,1,0:T(8,128)(2,1)} %get-tuple-element.13.queries.keys.values), custom_call_target="tpu_custom_call" | custom-call | flops 12079595520 | bytes 4194304 | tf_op jit(solution)/shard_map/encoder_attention/pallas_call | solution.py:117
  215.3 2.1 copy.35
  217.4 1.3 broadcast_select_fusion.5
  218.6 1.4 pad_maximum_fusion.1.out_w
  220.0 6.5 %collective-permute-done.1 = bf16[768,320]{0,1:T(8,128)(2,1)} collective-permute-done((bf16[768,320]{0,1:T(8,128)(2,1)}, bf16[768,320]{0,1:T(8,128)(2,1)}, u32[]{:S(2)}, u32[]{:S(2)}) %collective-permute-start.1) | collective-permute-done | bytes 491552 | tf_op jit(solution)/shard_map/ppermute | solution.py:465
  226.5 2.1 copy.36
  228.6 2.2 broadcast_select_fusion.6
  230.8 4.4 %broadcast_select_fusion = (bf16[1280,1024]{1,0:T(8,128)(2,1)}, bf16[1280,1024]{1,0:T(8,128)(2,1)}) fusion(bf16[1280,1024]{1,0:T(8,128)(2,1)} %collective-permute-done.3, pred[]{:T(512)S(6)} %eq.2, bf16[16,80,1024]{2,1,0:T(8,128)(2,1)S(1)} %copy-done), kind=kLoop, calls=%fused_computation.10 | loop fusion | flops 2621440 | bytes 10485761 | tf_op jit(solution)/shard_map/jit(_where)/select_n | solution.py:467
  235.2 17.3 %embed.1 = (bf16[896,2048]{1,0:T(8,128)(2,1)}, bf16[896,128]{1,0:T(8,128)(2,1)}) custom-call(f32[768,1280]{1,0:T(8,128)} %get-tuple-element.12.pooled, bf16[768,320]{1,0:T(8,128)(2,1)} %get-tuple-element.31.context_a, bf16[768,320]{1,0:T(8,128)(2,1)} %get-tuple-element.30.context_b, bf16[640,1280]{1,0:T(8,128)(2,1)} %pad_maximum_fusion.1.out_w, ...), custom_call_target="tpu_custom_call" | custom-call | flops 9395240960 | bytes 25165824 | tf_op jit(solution)/shard_map/embed/pallas_call | solution.py:167
  252.5 47.4 %decoder.1 = (f32[2,64,1024]{2,1,0:T(8,128)}, f32[128,2048]{1,0:T(8,128)}) custom-call(s32[1]{0:T(128)S(6)} %copy.51.count, bf16[896,2048]{1,0:T(8,128)(2,1)} %get-tuple-element.16.normed, bf16[896,128]{1,0:T(8,128)(2,1)} %get-tuple-element.17.low, bf16[16,384,1024]{2,1,0:T(8,128)(2,1)} %all-gather.2.cloned.1.call-done.weights, f32[2,64,1024]{2,1,0:T(8,128)} %up_w.1, ...), custom_call_target="tpu_custom_call" | custom-call | flops 18790481920 | bytes 25165824 | tf_op jit(solution)/shard_map/decoder/pallas_call | solution.py:276
  299.9 1.3 convert_element_type.51
  302.2 1.0 pad_maximum_fusion.2.terms
  303.2 58.5 %reduce_terms.1 = f32[192,128]{1,0:T(8,128)} custom-call(bf16[16,192,128]{2,1,0:T(8,128)(2,1)} %pad_maximum_fusion.2.terms), custom_call_target="tpu_custom_call" | custom-call | tf_op jit(solution)/shard_map/reduce_terms/pallas_call | solution.py:349
  361.7 0.8 slice.16
  362.6 0.8 slice.17
  (46 shorter events, 5.7 us)
Async XLA Ops:
  7.2 245.3 %all-gather.2.cloned.1.call-start = ((), (), s32[]{:S(2)}) async-start(), calls=%async_computation | async-start | bytes 13369344 | tf_op jit(solution)/shard_map/all_gather | solution.py:496
  7.2 84.9 %copy-start.5 = (bf16[1,21,2048]{2,1,0:T(8,128)(2,1)S(1)}, bf16[1,21,2048]{2,1,0:T(8,128)(2,1)}, u32[]{:S(2)}) copy-start(bf16[1,21,2048]{2,1,0:T(8,128)(2,1)} %param.27) | copy-start | bytes 258052
  7.2 84.9 %copy-start.6 = (f32[1280]{0:T(1024)S(1)}, f32[1280]{0:T(1024)}, u32[]{:S(2)}) copy-start(f32[1280]{0:T(1024)} %param.19) | copy-start | bytes 15364
  7.2 85.5 %copy-start.7 = (f32[1280]{0:T(1024)S(1)}, f32[1280]{0:T(1024)}, u32[]{:S(2)}) copy-start(f32[1280]{0:T(1024)} %param.20) | copy-start | bytes 15364
  7.9 155.5 %collective-permute-start = (bf16[750,1280]{1,0:T(8,128)(2,1)}, bf16[750,1280]{1,0:T(8,128)(2,1)}, u32[]{:S(2)}, u32[]{:S(2)}) collective-permute-start(bf16[750,1280]{1,0:T(8,128)(2,1)} %bitcast.31), channel_id=1, source_target_pairs={{0,1},{1,0},{2,3},{3,2},{4,5},{5,4},{6,7},{7,6},{8,9},{9,8},{10,11... | collective-permute-start | bytes 5760008 | tf_op jit(solution)/shard_map/ppermute | solution.py:465
  87.5 8.2 %copy-start.8 = (f32[1280]{0:T(1024)S(1)}, f32[1280]{0:T(1024)}, u32[]{:S(2)}) copy-start(f32[1280]{0:T(1024)} %param.23) | copy-start | bytes 15364
  87.5 8.8 %copy-start.9 = (f32[1280]{0:T(1024)S(1)}, f32[1280]{0:T(1024)}, u32[]{:S(2)}) copy-start(f32[1280]{0:T(1024)} %param.24) | copy-start | bytes 15364
  87.5 9.4 %copy-start.3 = (bf16[1,750,1024]{2,1,0:T(8,128)(2,1)S(1)}, bf16[1,750,1024]{2,1,0:T(8,128)(2,1)}, u32[]{:S(2)}) copy-start(bf16[1,750,1024]{2,1,0:T(8,128)(2,1)} %param.32) | copy-start | bytes 4608004
  90.0 127.4 %collective-permute-start.2 = (bf16[320,1280]{1,0:T(8,128)(2,1)S(1)}, bf16[320,1280]{1,0:T(8,128)(2,1)}, u32[]{:S(2)}, u32[]{:S(2)}) collective-permute-start(bf16[320,1280]{1,0:T(8,128)(2,1)S(1)} %copy.40), channel_id=1, source_target_pairs={{0,1},{1,0},{2,3},{3,2},{4,5},{5,4},{6,7},{7,6},{8,9},{9,8},{10,11... | collective-permute-start | bytes 2457608 | tf_op jit(solution)/shard_map/ppermute | solution.py:465
  90.1 140.8 %collective-permute-start.3 = (bf16[1280,1024]{1,0:T(8,128)(2,1)}, bf16[1280,1024]{1,0:T(8,128)(2,1)}, u32[]{:S(2)}, u32[]{:S(2)}) collective-permute-start(bf16[1280,1024]{1,0:T(8,128)(2,1)} %bitcast.28), channel_id=1, source_target_pairs={{0,1},{1,0},{2,3},{3,2},{4,5},{5,4},{6,7},{7,6},{8,9},{9,8},{10,11... | collective-permute-start | bytes 7864328 | tf_op jit(solution)/shard_map/ppermute | solution.py:465
  92.1 68.2 %collective-permute-start.4 = (bf16[21,2048]{1,0:T(8,128)(2,1)S(1)}, bf16[21,2048]{1,0:T(8,128)(2,1)}, u32[]{:S(2)}, u32[]{:S(2)}) collective-permute-start(bf16[21,2048]{1,0:T(8,128)(2,1)S(1)} %bitcast.38), channel_id=1, source_target_pairs={{0,1},{1,0},{2,3},{3,2},{4,5},{5,4},{6,7},{7,6},{8,9},{9,8},{10,11... | collective-permute-start | bytes 258056 | tf_op jit(solution)/shard_map/ppermute | solution.py:465
  103.4 59.9 %copy-start.2 = (bf16[1,750,1280]{2,1,0:T(8,128)(2,1)S(1)}, bf16[1,750,1280]{2,1,0:T(8,128)(2,1)}, u32[]{:S(2)}) copy-start(bf16[1,750,1280]{2,1,0:T(8,128)(2,1)} %param.17) | copy-start | bytes 5760004
  217.4 9.1 %collective-permute-start.1 = (bf16[768,320]{0,1:T(8,128)(2,1)}, bf16[768,320]{0,1:T(8,128)(2,1)}, u32[]{:S(2)}, u32[]{:S(2)}) collective-permute-start(bf16[768,320]{0,1:T(8,128)(2,1)} %copy.35), channel_id=1, source_target_pairs={{0,1},{1,0},{2,3},{3,2},{4,5},{5,4},{6,7},{7,6},{8,9},{9,8},{10,11... | collective-permute-start | bytes 1474568 | tf_op jit(solution)/shard_map/ppermute | solution.py:465
  218.6 10.0 %copy-start.1 = (bf16[768,320]{1,0:T(8,128)(2,1)S(1)}, bf16[768,320]{1,0:T(8,128)(2,1)}, u32[]{:S(2)}) copy-start(bf16[768,320]{1,0:T(8,128)(2,1)} %encoder_attention.1) | copy-start | bytes 1474564
  218.6 12.2 %copy-start = (bf16[16,80,1024]{2,1,0:T(8,128)(2,1)S(1)}, bf16[16,80,1024]{2,1,0:T(8,128)(2,1)}, u32[]{:S(2)}) copy-start(bf16[16,80,1024]{2,1,0:T(8,128)(2,1)} %get-tuple-element.15) | copy-start | bytes 7864324
  299.9 1.9 copy-start.4
Sparse Core Ops, SparseCore 0:
  10.3 117.7 all-gather.1

commit v4 on v3

--- a/solution.py
+++ b/solution.py
@@ -109,6 +109,8 @@
         total_weight = jnp.sum(weights, -1, keepdims=True)
         context = dot(weights.astype(BF16), values[0, :, span]) / total_weight
         out[:, span] = dot(pairs, context.astype(BF16)).astype(BF16)
+    if out.shape[1] > columns:
+        out[:, columns:] = jnp.zeros((tile // 2, out.shape[1] - columns), BF16)
 
 
 def encoder_attention(triple, count):
@@ -123,8 +125,8 @@
             pl.BlockSpec((1, padded, columns), lambda i: (1, 0, 0)),
             pl.BlockSpec((1, padded, columns), lambda i: (2, 0, 0)),
         ],
-        out_specs=pl.BlockSpec((tile // 2, columns), lambda i: (i, 0)),
-        out_shape=jax.ShapeDtypeStruct((padded // 2, columns), BF16),
+        out_specs=pl.BlockSpec((tile // 2, round_up(columns, 128)), lambda i: (i, 0)),
+        out_shape=jax.ShapeDtypeStruct((padded // 2, round_up(columns, 128)), BF16),
         compiler_params=params(),
         cost_estimate=pl.CostEstimate(
             flops=16 * padded * padded * columns,
@@ -136,16 +138,20 @@
 
 
 def embed_kernel(
-    audio, pooled, context_a, context_b, out_w, gain, shift, proj_a, proj_b, proj_shift,
-    text, root_gain, low_w, normed_out, low_out,
+    audio, pooled, context_a, context_b, out_a, out_b, gain, shift, a_top, a_end, b_top, b_end,
+    proj_shift, text, root_gain, low_w, normed_out, low_out,
 ):
     tile = pooled.shape[0]
-    half = out_w.shape[0] // 2
-    hidden = pooled[...] + dot(context_a[...], out_w[:half]) + dot(context_b[...], out_w[half:])
+    heads = out_a.shape[0]
+    hidden = (
+        pooled[...] + dot(context_a[:, :heads], out_a[...]) + dot(context_b[:, :heads], out_b[...])
+    )
     pooled_norm = layer_norm(hidden, gain[...], shift[...]).astype(BF16)
-    columns = proj_a.shape[1]
-    first = (dot(pooled_norm, proj_a[...]) + proj_shift[:, :columns]).astype(BF16)
-    second = (dot(pooled_norm, proj_b[...]) + proj_shift[:, columns:]).astype(BF16)
+    half, columns = a_top.shape
+    left, right = pooled_norm[:, :half], pooled_norm[:, half:]
+    first = dot(left, a_top[...]) + dot(right, a_end[...]) + proj_shift[:, :columns]
+    second = dot(left, b_top[...]) + dot(right, b_end[...]) + proj_shift[:, columns:]
+    first, second = first.astype(BF16), second.astype(BF16)
     embedded = jnp.concatenate([first, second], 1).astype(F32)
     index = lax.broadcasted_iota(jnp.int32, (tile, 1), 0) + pl.program_id(0) * tile
     rows = jnp.where(index < audio, embedded, text[...].astype(F32))
@@ -155,8 +161,8 @@
     low_out[...] = dot(normed, low_w[...]).astype(BF16)
 
 
-def embed(audio, pooled, context_a, context_b, out_w, gain, shift, proj_a, proj_b, proj_shift,
-          text, root_gain, low_w):
+def embed(audio, pooled, context_a, context_b, out_a, out_b, gain, shift, projections,
+          proj_shift, text, root_gain, low_w):
     total, features = text.shape
     width = pooled.shape[1]
     tile = total // 2
@@ -171,11 +177,11 @@
             pl.BlockSpec((tile, width), held),
             pl.BlockSpec((tile, context_a.shape[1]), held),
             pl.BlockSpec((tile, context_b.shape[1]), held),
-            whole(out_w.shape),
+            whole(out_a.shape),
+            whole(out_b.shape),
             whole((1, width)),
             whole((1, width)),
-            whole(proj_a.shape),
-            whole(proj_b.shape),
+            *[whole(p.shape) for p in projections],
             whole((1, features)),
             pl.BlockSpec((tile, features), row),
             whole((1, features)),
@@ -194,7 +200,7 @@
             flops=2 * total * width * features * 2, bytes_accessed=24 * 2**20, transcendentals=0
         ),
         name="embed",
-    )(pooled, context_a, context_b, out_w, gain[None], shift[None], proj_a, proj_b,
+    )(pooled, context_a, context_b, out_a, out_b, gain[None], shift[None], *projections,
       proj_shift[None], text, root_gain[None], low_w)
 
 
@@ -467,6 +473,22 @@
     return jnp.where(first, value, other), jnp.where(first, other, value)
 
 
+def swap(value):
+    return lax.ppermute(value, "tensor", [(0, 1), (1, 0)])
+
+
+def other_half(value):
+    half = value.shape[0] // 2
+    core = lax.rem(lax.axis_index("dp"), 2)
+    return swap(lax.dynamic_slice_in_dim(value, core * half, half, 0))
+
+
+def other_halves(got):
+    core = lax.rem(lax.axis_index("dp"), 2)
+    mate = lax.ppermute(got, "dp", [(i, i ^ 1) for i in range(lax.axis_size("dp"))])
+    return jnp.where(core == 0, got, mate), jnp.where(core == 0, mate, got)
+
+
 def per_device(
     frames,
     frame_counts,
@@ -502,8 +524,11 @@
         encoder_w, out_parts, proj_parts = [lax.all_gather(s, "dp") for s in shards]
         encoder_w = encoder_w.transpose(1, 0, 2, 3).reshape(1, 3, -1, encoder_w.shape[3])
     out_half = out_parts.transpose(1, 0, 2).reshape(encoder_out.shape[0], -1)
-    proj_a, proj_b = both(proj_parts.reshape(-1, columns), 1)
-    out_w = jnp.concatenate(both(out_half, 0), 0)
+    proj = proj_parts.reshape(-1, columns)
+    first = lax.axis_index("tensor") == 0
+    top, end = proj[: proj.shape[0] // 2], proj[proj.shape[0] // 2:]
+    proj_got = other_half(proj)
+    out_got = other_half(out_half)
     text = jnp.concatenate(both(text_embed[0], 0), 0)
     text = jnp.pad(text, ((audio, tail), (0, 0)))
     upstream = jnp.pad(
@@ -511,11 +536,20 @@
     )
     triple, pooled = encode(all_frames, encoder_gain, encoder_shift, encoder_w)
     context = encoder_attention(triple, frame_counts)
-    context_a, context_b = both(context, 1)
+    context, proj_got, out_got = lax.optimization_barrier((context, proj_got, out_got))
+    context_other = swap(context)
+    other_top, other_end = other_halves(proj_got)
+    projections = [
+        jnp.where(first, top, other_top),
+        jnp.where(first, end, other_end),
+        jnp.where(first, other_top, top),
+        jnp.where(first, other_end, end),
+    ]
+    out_other = jnp.concatenate(other_halves(out_got), 0)
     low_w = jnp.concatenate([adapter_in[0], adapter_in[1]], 1).astype(BF16)
     normed, low = embed(
-        audio, pooled, context_a, context_b, out_w, post_gain, post_shift, proj_a, proj_b,
-        projector_shift, text, decoder_gain, low_w,
+        audio, pooled, context, context_other, out_half, out_other, post_gain, post_shift,
+        projections, projector_shift, text, decoder_gain, low_w,
     )
     cosine, sine = rope_tables(total)
     grads_out, grads_in = decoder(

time: 375 us -> 362 us (0.965)
  starting transfers between devices: 5.24 us -> 20.3 us
  Pallas kernels: 246 us -> 231 us
  waiting for transfers between devices: 64 us -> 53.4 us
  other arithmetic: 25.4 us -> 20.2 us
    ppermute x5 -> x2, waiting for transfers between devices: 63.4 us -> 43.7 us  [both(): other = lax.ppermute(value, 'tensor', [(0, 1), (1, 0)])]
    ppermute x0 -> x5, starting transfers between devices: none -> 19.4 us  [the longest x2 14.6 us: other_halves(): lax.ppermute(got, 'dp', [(i, i ^ 1) for i in range(lax.axis_size('dp'))])]
    pallas_call x1, Pallas kernels: 58.5 us -> 44.3 us  [reduce_terms(): pl.pallas_call(functools.partial(reduce_kernel, parts, shared), out_shape...]
    ppermute x0 -> x5, waiting for transfers between devices: none -> 8.97 us  [the longest x3 8.96 us: swap(): return lax.ppermute(value, 'tensor', [(0, 1), (1, 0)])]
    select_n x5 -> x2, other arithmetic: 10.8 us -> 2.69 us  [both(): return (jnp.where(first, value, other), jnp.where(first, other, value))]
    ppermute x5 -> x2, starting transfers between devices: 5.2 us -> 0.84 us  [both(): other = lax.ppermute(value, 'tensor', [(0, 1), (1, 0)])]
    dynamic_slice x0 -> x2, local copies, waits for them, and re-layouts: none -> 4.3 us  [other_half(): return swap(lax.dynamic_slice_in_dim(value, core * half, half, 0))]
    select_n x0 -> x2, other arithmetic: none -> 4.18 us  [the longest x1 4.12 us: per_device(): jnp.where(first, other_end, end)]
  transfers between devices with their start and end apart: 6 -> 8, of which waited for: 2 -> 2; matrix products, arithmetic and copies ran while one was open for 10% -> 9% of each run, Pallas kernels for 38% -> 39%
where the time goes in v4:
time: 362 us; the launch traced here: 359 us
  Pallas kernels  231 us (64%)
  waiting for transfers between devices  53.4 us (15%)
  starting transfers between devices  20.3 us (6%)
  other arithmetic  20.2 us (6%)
  local copies, waits for them, and re-layouts  18.9 us (5%)
  between operations  14.9 us (4%)
    pallas_call x1, Pallas kernels, ring_gather(): pl.pallas_call(functools.partial(ring_kernel, parts, count), out_shape=[j...  74 us
    pallas_call x1, Pallas kernels, decoder(): pl.pallas_call(functools.partial(decoder_kernel, audio), grid=(all_column...  47.5 us
    pallas_call x1, Pallas kernels, reduce_terms(): pl.pallas_call(functools.partial(reduce_kernel, parts, shared), out_shape...  44.3 us
    ppermute x2, waiting for transfers between devices, both(): other = lax.ppermute(value, 'tensor', [(0, 1), (1, 0)])  43.7 us
    pallas_call x1, Pallas kernels, encoder_attention(): pl.pallas_call(encoder_attention_kernel, grid=(padded // tile,), in_specs...  34.5 us
    pallas_call x1, Pallas kernels, embed(): pl.pallas_call(functools.partial(embed_kernel, audio), grid=(total // til...  18.2 us
    ppermute x2, starting transfers between devices, other_halves(): lax.ppermute(got, 'dp', [(i, i ^ 1) for i in range(lax.axis_size('dp'))])  14.6 us
    pallas_call x1, Pallas kernels, encode(): pl.pallas_call(functools.partial(encode_kernel, length), grid=(padded //...  13 us
  transfers between devices with their start and end apart: 8, of which 2 were waited for; matrix products, arithmetic and copies ran while one was open for 9% of the time, Pallas kernels for 39%

profile of v4, /device:TPU:0, one launch (start us, length us, event | category | flops | bytes accessed | tf_op | source)
XLA Modules:
  0.0 359.1 jit_solution(2922801528527750876)
XLA Ops:
  7.9 1.6 copy.33.refs_1_
  9.5 74.0 %ring_gather.1 = (bf16[16,3,80,320]{3,2,1,0:T(8,128)(2,1)}, bf16[16,320,80]{2,1,0:T(8,128)(2,1)}, bf16[16,80,1024]{2,1,0:T(8,128)(2,1)}) custom-call(bf16[3,80,320]{2,1,0:T(8,128)(2,1)} %refs_0_.1, bf16[320,80]{1,0:T(8,128)(2,1)} %copy.33.refs_1_, bf16[80,1024]{1,0:T(8,128)(2,1)} %refs_2_.1), custom_call_target="tpu_custom_call" | custom-call | bytes 134217728 | tf_op jit(solution)/shard_map/ring_gather/pallas_call | solution.py:444
  83.4 2.5 constant_dynamic-slice_fusion.2
  85.9 1.6 collective-permute-start.1
  88.0 1.8 copy.34
  89.7 1.3 copy.35.out_a
  91.0 1.8 constant_dynamic-slice_fusion.1
  92.9 1.6 collective-permute-start.2
  96.7 1.7 copy.36
  99.7 1.7 fusion.7
  101.4 1.2 pad_maximum_fusion.4
  102.6 1.4 fusion.6.upstream
  104.1 1.1 pad_maximum_fusion.3.low_w
  106.3 43.7 %collective-permute-done = bf16[750,1280]{1,0:T(8,128)(2,1)} collective-permute-done((bf16[750,1280]{1,0:T(8,128)(2,1)S(1)}, bf16[750,1280]{1,0:T(8,128)(2,1)}, u32[]{:S(2)}, u32[]{:S(2)}) %collective-permute-start) | collective-permute-done | bytes 1920032 | tf_op jit(solution)/shard_map/ppermute | solution.py:471
  150.0 1.8 broadcast_select_fusion.1
  151.8 2.3 pad_maximum_fusion.frames
  154.1 13.0 %encode.1 = (bf16[3,1536,320]{2,1,0:T(8,128)(2,1)}, f32[768,1280]{1,0:T(8,128)}) custom-call(bf16[1500,1280]{1,0:T(8,128)(2,1)} %pad_maximum_fusion.frames, f32[1,1280]{1,0:T(1,128)} %broadcast_in_dim.20.gain, f32[1,1280]{1,0:T(1,128)} %broadcast_in_dim.21.shift, bf16[16,3,80,320]{3,2,1,0:T(8,128)(2,1)} %get-tuple-element.14.weights), custom_call_target="tpu_custom_call" | custom-call | flops 3774873600 | bytes 14680064 | tf_op jit(solution)/shard_map/encode/pallas_call | solution.py:74
  167.1 34.5 %encoder_attention.1.context_a = bf16[768,384]{1,0:T(8,128)(2,1)} custom-call(s32[1]{0:T(128)S(6)} %copy.46.count, bf16[3,1536,320]{2,1,0:T(8,128)(2,1)} %get-tuple-element.16.queries.keys.values, bf16[3,1536,320]{2,1,0:T(8,128)(2,1)} %get-tuple-element.16.queries.keys.values, bf16[3,1536,320]{2,1,0:T(8,128)(2,1)} %get-tuple-element.16.queries.keys.values), custom_call_target="tpu_custom_call" | custom-call | flops 12079595520 | bytes 4194304 | tf_op jit(solution)/shard_map/encoder_attention/pallas_call | solution.py:119
  201.7 14.5 %collective-permute-start.5 = (bf16[640,1024]{1,0:T(8,128)(2,1)}, bf16[640,1024]{1,0:T(8,128)(2,1)S(1)}, u32[]{:S(2)}, u32[]{:S(2)}) collective-permute-start(bf16[640,1024]{1,0:T(8,128)(2,1)} %collective-permute-done.1), channel_id=1, source_target_pairs={{0,2},{2,0},{4,6},{6,4},{8,10},{10,8},{12,14},{14,12},{16,18},{18,... | collective-permute-start | bytes 3932168 | tf_op jit(solution)/shard_map/ppermute | solution.py:488
  216.1 0.9 broadcast_select_fusion.7
  217.2 2.2 fusion.3.text
  219.3 1.6 collective-permute-start.3
  221.0 1.0 pad_maximum_fusion.1.out_b
  222.0 4.1 %bitcast_select_fusion = (bf16[640,1024]{1,0:T(8,128)(2,1)}, bf16[640,1024]{1,0:T(8,128)(2,1)}, bf16[640,1024]{1,0:T(8,128)(2,1)}, bf16[640,1024]{1,0:T(8,128)(2,1)}) fusion(bf16[8,80,1024]{2,1,0:T(8,128)(2,1)S(1)} %get-tuple-element.38, pred[]{:T(512)S(6)} %eq.4, bf16[640,1024]{1,0:T(8,128)(2,1)S(1)} %collective-permute-done.5, ...), kind=kLoop, calls=%fused_computation.13 | loop fusion | flops 3932160 | bytes 10485762 | tf_op jit(solution)/shard_map/jit(_where)/select_n | solution.py:546
  226.1 9.0 %collective-permute-done.3.context_b = bf16[768,384]{1,0:T(8,128)(2,1)S(1)} collective-permute-done((bf16[768,384]{1,0:T(8,128)(2,1)S(1)}, bf16[768,384]{1,0:T(8,128)(2,1)S(1)}, u32[]{:S(2)}, u32[]{:S(2)}) %collective-permute-start.3) | collective-permute-done | bytes 589856 | tf_op jit(solution)/shard_map/ppermute | solution.py:477
  235.0 0.8 copy-done.11
  235.9 18.2 %embed.1 = (bf16[896,2048]{1,0:T(8,128)(2,1)}, bf16[896,128]{1,0:T(8,128)(2,1)}) custom-call(f32[768,1280]{1,0:T(8,128)} %get-tuple-element.15.pooled, bf16[768,384]{1,0:T(8,128)(2,1)} %encoder_attention.1.context_a, bf16[768,384]{1,0:T(8,128)(2,1)} %copy-done.11, bf16[320,1280]{1,0:T(8,128)(2,1)} %copy.35.out_a, bf16[320,1280]{1,0:T(8,128)(2,1)} %pad_maximum_fusion.1.out_b, ...), custom_call_target="tpu_custom_call" | custom-call | flops 9395240960 | bytes 25165824 | tf_op jit(solution)/shard_map/embed/pallas_call | solution.py:173
  254.1 47.5 %decoder.1 = (f32[2,64,1024]{2,1,0:T(8,128)}, f32[128,2048]{1,0:T(8,128)}) custom-call(s32[1]{0:T(128)S(6)} %copy.46.count, bf16[896,2048]{1,0:T(8,128)(2,1)} %get-tuple-element.22.normed, bf16[896,128]{1,0:T(8,128)(2,1)} %get-tuple-element.23.low, bf16[16,384,1024]{2,1,0:T(8,128)(2,1)} %all-gather.2.cloned.1.call-done.weights, f32[2,64,1024]{2,1,0:T(8,128)} %up_w.1, ...), custom_call_target="tpu_custom_call" | custom-call | flops 18790481920 | bytes 25165824 | tf_op jit(solution)/shard_map/decoder/pallas_call | solution.py:282
  301.6 1.3 convert_element_type.51
  303.9 1.0 pad_maximum_fusion.2.terms
  304.9 44.3 %reduce_terms.1 = f32[192,128]{1,0:T(8,128)} custom-call(bf16[16,192,128]{2,1,0:T(8,128)(2,1)} %pad_maximum_fusion.2.terms), custom_call_target="tpu_custom_call" | custom-call | tf_op jit(solution)/shard_map/reduce_terms/pallas_call | solution.py:355
  349.2 0.8 slice.32
  (54 shorter events, 8.4 us)
Async XLA Ops:
  7.2 247.0 %all-gather.2.cloned.1.call-start = ((), (), s32[]{:S(2)}) async-start(), calls=%async_computation | async-start | bytes 13369344 | tf_op jit(solution)/shard_map/all_gather | solution.py:518
  7.2 80.3 %copy-start.1 = (bf16[1,750,1280]{2,1,0:T(8,128)(2,1)S(1)}, bf16[1,750,1280]{2,1,0:T(8,128)(2,1)}, u32[]{:S(2)}) copy-start(bf16[1,750,1280]{2,1,0:T(8,128)(2,1)} %param.17) | copy-start | bytes 5760004
  85.9 115.7 %collective-permute-start.1 = (bf16[640,1024]{1,0:T(8,128)(2,1)}, bf16[640,1024]{1,0:T(8,128)(2,1)}, u32[]{:S(2)}, u32[]{:S(2)}) collective-permute-start(bf16[640,1024]{1,0:T(8,128)(2,1)} %constant_dynamic-slice_fusion.2), channel_id=1, source_target_pairs={{0,1},{1,0},{2,3},{3,2},{4,5},{5,4},{6,7},{7,6},{8,9},{9,8},{10,11... | collective-permute-start | bytes 3932168 | tf_op jit(solution)/shard_map/ppermute | solution.py:477
  87.5 62.5 %collective-permute-start = (bf16[750,1280]{1,0:T(8,128)(2,1)S(1)}, bf16[750,1280]{1,0:T(8,128)(2,1)}, u32[]{:S(2)}, u32[]{:S(2)}) collective-permute-start(bf16[750,1280]{1,0:T(8,128)(2,1)S(1)} %bitcast.35), channel_id=1, source_target_pairs={{0,1},{1,0},{2,3},{3,2},{4,5},{5,4},{6,7},{7,6},{8,9},{9,8},{10,11... | collective-permute-start | bytes 5760008 | tf_op jit(solution)/shard_map/ppermute | solution.py:471
  88.0 6.5 %copy-start.4 = (bf16[1,21,2048]{2,1,0:T(8,128)(2,1)S(1)}, bf16[1,21,2048]{2,1,0:T(8,128)(2,1)}, u32[]{:S(2)}) copy-start(bf16[1,21,2048]{2,1,0:T(8,128)(2,1)} %param.27) | copy-start | bytes 258052
  88.0 6.9 %copy-start.6 = (f32[1280]{0:T(1024)S(1)}, f32[1280]{0:T(1024)}, u32[]{:S(2)}) copy-start(f32[1280]{0:T(1024)} %param.19) | copy-start | bytes 15364
  88.0 7.5 %copy-start.7 = (f32[1280]{0:T(1024)S(1)}, f32[1280]{0:T(1024)}, u32[]{:S(2)}) copy-start(f32[1280]{0:T(1024)} %param.20) | copy-start | bytes 15364
  91.0 7.4 %copy-start.8 = (f32[1280]{0:T(1024)S(1)}, f32[1280]{0:T(1024)}, u32[]{:S(2)}) copy-start(f32[1280]{0:T(1024)} %param.23) | copy-start | bytes 15364
  91.0 8.0 %copy-start.9 = (f32[1280]{0:T(1024)S(1)}, f32[1280]{0:T(1024)}, u32[]{:S(2)}) copy-start(f32[1280]{0:T(1024)} %param.24) | copy-start | bytes 15364
  92.9 108.8 %collective-permute-start.2 = (bf16[160,1280]{1,0:T(8,128)(2,1)}, bf16[160,1280]{1,0:T(8,128)(2,1)S(1)}, u32[]{:S(2)}, u32[]{:S(2)}) collective-permute-start(bf16[160,1280]{1,0:T(8,128)(2,1)} %constant_dynamic-slice_fusion.1), channel_id=1, source_target_pairs={{0,1},{1,0},{2,3},{3,2},{4,5},{5,4},{6,7},{7,6},{8,9},{9,8},{10,11... | collective-permute-start | bytes 1228808 | tf_op jit(solution)/shard_map/ppermute | solution.py:477
  94.5 121.7 %collective-permute-start.6 = (bf16[21,2048]{1,0:T(8,128)(2,1)S(1)}, bf16[21,2048]{1,0:T(8,128)(2,1)}, u32[]{:S(2)}, u32[]{:S(2)}) collective-permute-start(bf16[21,2048]{1,0:T(8,128)(2,1)S(1)} %bitcast.42), channel_id=1, source_target_pairs={{0,1},{1,0},{2,3},{3,2},{4,5},{5,4},{6,7},{7,6},{8,9},{9,8},{10,11... | collective-permute-start | bytes 258056 | tf_op jit(solution)/shard_map/ppermute | solution.py:471
  99.7 3.0 copy-start.2
  99.7 3.0 copy-start.5
  104.1 1.9 copy-start
  201.7 20.3 %collective-permute-start.5 = (bf16[640,1024]{1,0:T(8,128)(2,1)}, bf16[640,1024]{1,0:T(8,128)(2,1)S(1)}, u32[]{:S(2)}, u32[]{:S(2)}) collective-permute-start(bf16[640,1024]{1,0:T(8,128)(2,1)} %collective-permute-done.1), channel_id=1, source_target_pairs={{0,2},{2,0},{4,6},{6,4},{8,10},{10,8},{12,14},{14,12},{16,18},{18,... | collective-permute-start | bytes 3932168 | tf_op jit(solution)/shard_map/ppermute | solution.py:488
  217.1 3.9 %collective-permute-start.4 = (bf16[160,1280]{1,0:T(8,128)(2,1)S(1)}, bf16[160,1280]{1,0:T(8,128)(2,1)S(1)}, u32[]{:S(2)}, u32[]{:S(2)}) collective-permute-start(bf16[160,1280]{1,0:T(8,128)(2,1)S(1)} %collective-permute-done.2), channel_id=1, source_target_pairs={{0,2},{2,0},{4,6},{6,4},{8,10},{10,8},{12,14},{14,12},{16,18},{18,... | collective-permute-start | bytes 1228808 | tf_op jit(solution)/shard_map/ppermute | solution.py:488
  217.2 2.2 copy-start.10
  219.3 15.7 %collective-permute-start.3 = (bf16[768,384]{1,0:T(8,128)(2,1)S(1)}, bf16[768,384]{1,0:T(8,128)(2,1)S(1)}, u32[]{:S(2)}, u32[]{:S(2)}) collective-permute-start(bf16[768,384]{1,0:T(8,128)(2,1)S(1)} %copy-done.10), channel_id=1, source_target_pairs={{0,1},{1,0},{2,3},{3,2},{4,5},{5,4},{6,7},{7,6},{8,9},{9,8},{10,11... | collective-permute-start | bytes 1769480 | tf_op jit(solution)/shard_map/ppermute | solution.py:477
  235.0 0.8 copy-start.11
  301.6 1.9 copy-start.3
Sparse Core Ops, SparseCore 0:
  10.3 116.2 all-gather.1
